TPU v7x, 32 devices: a whole 2x2x4 slice. The times are simulated.
32 devices in a mesh: fine: 16 (over z, x, core), coarse: 2 (over y).
Axes of the slice: x: 2, y: 2, z: 4, core: 2. Of those that a mesh axis runs over, the one named last changes fastest.
Arguments:
- start_states: float32 [16, 1, 16, 64, 256], P('fine', None, 'coarse'), may hold values from -6 to 6
- weights: bfloat16 [64, 9, 256, 256], P('fine'), may hold values from -0.125 to 0.125
- biases: float32 [64, 256], P('fine'), may hold values from -3 to 3
- step_sizes: float32 [64], P('fine'), may hold values from 0.1 to 0.4
Outputs:
- corrected: float32 [16, 1, 16, 64, 256], P('fine', None, 'coarse')
- slab_ends: float32 [16, 1, 16, 64, 256], P('fine', None, 'coarse')
All inputs are finite; a program needn't handle non-finite values.
Results may differ from a plain program's by a relative error of at most 0.014.
Values may be sent and summed in bfloat16 or wider, within the bound.
A program may use at most 64 MiB of HBM per device.

v0:
```python
import jax
import jax.numpy as jnp
from jax import lax
from jax.sharding import PartitionSpec as P


def extended_2(cells, sides, width):
    for axis, dim in sides:
        count = lax.axis_size(axis)
        ends = count - 1
        head = lax.slice_in_dim(cells, 0, width, axis=dim)
        tail = lax.slice_in_dim(cells, cells.shape[dim] - width, cells.shape[dim], axis=dim)
        cells = jnp.concatenate(
            [
                lax.ppermute(tail, axis, [(i, (i + 1) % count) for i in range(ends)]),
                cells,
                lax.ppermute(head, axis, [((i + 1) % count, i) for i in range(ends)]),
            ],
            axis=dim,
        )
    return cells


def from_behind(array, axis, by):
    count = lax.axis_size(axis)
    pairs = [(i, i + by) for i in range(count) if 0 <= i + by < count]
    return lax.ppermute(array, axis, pairs)


def conv_rows(padded, kernel):
    widened = jnp.pad(padded, ((0, 0), (0, 0), (1, 1), (0, 0)))
    row_count = padded.shape[1] - 2
    col_count = padded.shape[2]
    channels = padded.shape[3]
    tap_slices = [
        widened[:, row_shift : row_shift + row_count, col_shift : col_shift + col_count, :]
        for row_shift in range(3)
        for col_shift in range(3)
    ]
    stacked = jnp.concatenate(tap_slices, axis=-1).reshape(-1, 9 * channels)
    product = jnp.dot(
        stacked, kernel.reshape(9 * channels, channels), preferred_element_type=jnp.float32
    )
    return product.reshape(padded.shape[0], row_count, col_count, channels)


def relax(current_state, weights, biases, step_sizes):
    layer_count = weights.shape[0]
    row_count = current_state.shape[1]
    first_slope = jnp.zeros(current_state.shape, jnp.float32)
    extended = extended_2(current_state, (("coarse", 1),), layer_count)
    all_rows = row_count * lax.axis_size("coarse")
    row_start = lax.axis_index("coarse") * row_count
    for layer_index in range(layer_count):
        margin = layer_count - layer_index - 1
        slope_term = jnp.tanh(
            conv_rows(extended.astype(jnp.bfloat16), weights[layer_index]) + biases[layer_index]
        )
        extended = extended[:, 1:-1] + step_sizes[layer_index] * slope_term
        position = row_start - margin + jnp.arange(extended.shape[1], dtype=jnp.int32)
        inside = (position >= 0) & (position < all_rows)
        extended = jnp.where(inside[None, :, None, None], extended, 0.0)
        if layer_index == 0:
            first_slope = slope_term[:, margin : margin + row_count]
    return (extended, first_slope)


def local(start_states, weights, biases, step_sizes):
    initial = start_states[0]
    relaxed, first_slope = relax(initial, weights, biases, step_sizes)
    coarse_step = jnp.sum(step_sizes)
    defect = relaxed - (initial + coarse_step * first_slope)
    slab_index = lax.axis_index("fine")
    slab_count = lax.axis_size("fine")

    def turn(turn_index, carried):
        padded = extended_2(carried.astype(jnp.bfloat16), (("coarse", 1),), 1)
        slope_term = lax.cond(
            slab_index == turn_index,
            lambda: jnp.tanh(conv_rows(padded, weights[0]) + biases[0]),
            lambda: jnp.zeros(carried.shape, jnp.float32),
        )
        advanced = carried + coarse_step * slope_term + defect
        arrived = from_behind(advanced, "fine", 1)
        return jnp.where(slab_index == turn_index + 1, arrived, carried)

    corrected = lax.fori_loop(0, slab_count - 1, turn, initial)
    finished, unused = relax(corrected, weights, biases, step_sizes)
    return (corrected[None], finished[None])


def solution(mesh):
    in_specs = (
        P("fine", None, "coarse", None, None),
        P("fine", None, None, None),
        P("fine", None),
        P("fine"),
    )
    out_specs = (P("fine", None, "coarse", None, None), P("fine", None, "coarse", None, None))
    return jax.shard_map(local, mesh=mesh, in_specs=in_specs, out_specs=out_specs, check_vma=False)
```

profile of v0, /device:TPU:24, one launch (start us, length us, event | category | flops | bytes accessed | tf_op | source)
XLA Modules:
  0.0 353.2 jit_solution(15209757836965585061)
XLA Ops:
  2.5 3.4 collective-permute-start.3
  8.8 4.1 %fusion.165 = (bf16[1,9,256,256]{3,2,1,0:T(8,128)(2,1)}, bf16[1,9,256,256]{3,2,1,0:T(8,128)(2,1)S(1)}, bf16[1,9,256,256]{3,2,1,0:T(8,128)(2,1)}, bf16[1,9,256,256]{3,2,1,0:T(8,128)(2,1)S(1)}) fusion(bf16[4,9,256,256]{3,2,1,0:T(8,128)(2,1)} %param.9), kind=kLoop, calls=%fused_computation.166 | loop fusion | bytes 9437184 | tf_op jit(solution)/shard_map/slice | solution.py:57
  13.7 2.1 collective-permute-done.4
  25.4 2.1 fusion.141
  27.5 300.7 %while.13 = (s32[]{:T(128)}, f32[1,8,64,256]{3,2,1,0:T(8,128)S(1)}, s32[]{:T(128)}, f32[]{:T(128)}, bf16[4,9,256,256]{3,2,1,0:T(8,128)(2,1)}, /*index=5*/f32[4,2...) while((s32[]{:T(128)}, f32[1,8,64,256]{3,2,1,0:T(8,128)S(1)}, s32[]{:T(128)}, f32[]{:T(128)}, ...), condition=%wide.region_4.5_spmd, body=%wide.region_1.4_spmd.sunk | while | flops 605093888 | bytes 19139848 | solution.py:87
  28.9 4.5 %collective-permute-start.1 = (bf16[1,1,64,256]{3,2,1,0:T(8,128)(2,1)S(1)}, bf16[1,1,64,256]{3,2,1,0:T(8,128)(2,1)S(1)}, u32[]{:S(2)}, u32[]{:S(2)}) collective-permute-start(bf16[1,1,64,256]{3,2,1,0:T(8,128)(2,1)S(1)} %get-tuple-element.234), channel_id=1, source_target_pairs={{0,1},{2,3},{4,5},{6,7},{8,9},{10,11},{12,13},{14,15},{16,17},{18,... | collective-permute-start | bytes 98312 | tf_op jit(solution)/shard_map/while/body/eval_jaxpr/ppermute | solution.py:15
  35.8 1.9 collective-permute-start.2
  37.8 9.5 %collective-permute-done.2 = f32[1,8,64,256]{3,2,1,0:T(8,128)S(1)} collective-permute-done((f32[1,8,64,256]{3,2,1,0:T(8,128)S(1)}, f32[1,8,64,256]{3,2,1,0:T(8,128)S(1)}, u32[]{:S(2)}, u32[]{:S(2)}) %collective-permute-start.2) | collective-permute-done | bytes 524320 | tf_op jit(solution)/shard_map/while/body/eval_jaxpr/ppermute | solution.py:27
  48.7 4.5 %collective-permute-start.1 = (bf16[1,1,64,256]{3,2,1,0:T(8,128)(2,1)S(1)}, bf16[1,1,64,256]{3,2,1,0:T(8,128)(2,1)S(1)}, u32[]{:S(2)}, u32[]{:S(2)}) collective-permute-start(bf16[1,1,64,256]{3,2,1,0:T(8,128)(2,1)S(1)} %get-tuple-element.234), channel_id=1, source_target_pairs={{0,1},{2,3},{4,5},{6,7},{8,9},{10,11},{12,13},{14,15},{16,17},{18,... | collective-permute-start | bytes 98312 | tf_op jit(solution)/shard_map/while/body/eval_jaxpr/ppermute | solution.py:15
  55.7 1.9 collective-permute-start.2
  57.6 9.5 %collective-permute-done.2 = f32[1,8,64,256]{3,2,1,0:T(8,128)S(1)} collective-permute-done((f32[1,8,64,256]{3,2,1,0:T(8,128)S(1)}, f32[1,8,64,256]{3,2,1,0:T(8,128)S(1)}, u32[]{:S(2)}, u32[]{:S(2)}) %collective-permute-start.2) | collective-permute-done | bytes 524320 | tf_op jit(solution)/shard_map/while/body/eval_jaxpr/ppermute | solution.py:27
  68.6 4.5 %collective-permute-start.1 = (bf16[1,1,64,256]{3,2,1,0:T(8,128)(2,1)S(1)}, bf16[1,1,64,256]{3,2,1,0:T(8,128)(2,1)S(1)}, u32[]{:S(2)}, u32[]{:S(2)}) collective-permute-start(bf16[1,1,64,256]{3,2,1,0:T(8,128)(2,1)S(1)} %get-tuple-element.234), channel_id=1, source_target_pairs={{0,1},{2,3},{4,5},{6,7},{8,9},{10,11},{12,13},{14,15},{16,17},{18,... | collective-permute-start | bytes 98312 | tf_op jit(solution)/shard_map/while/body/eval_jaxpr/ppermute | solution.py:15
  75.6 1.9 collective-permute-start.2
  77.5 9.5 %collective-permute-done.2 = f32[1,8,64,256]{3,2,1,0:T(8,128)S(1)} collective-permute-done((f32[1,8,64,256]{3,2,1,0:T(8,128)S(1)}, f32[1,8,64,256]{3,2,1,0:T(8,128)S(1)}, u32[]{:S(2)}, u32[]{:S(2)}) %collective-permute-start.2) | collective-permute-done | bytes 524320 | tf_op jit(solution)/shard_map/while/body/eval_jaxpr/ppermute | solution.py:27
  88.5 4.5 %collective-permute-start.1 = (bf16[1,1,64,256]{3,2,1,0:T(8,128)(2,1)S(1)}, bf16[1,1,64,256]{3,2,1,0:T(8,128)(2,1)S(1)}, u32[]{:S(2)}, u32[]{:S(2)}) collective-permute-start(bf16[1,1,64,256]{3,2,1,0:T(8,128)(2,1)S(1)} %get-tuple-element.234), channel_id=1, source_target_pairs={{0,1},{2,3},{4,5},{6,7},{8,9},{10,11},{12,13},{14,15},{16,17},{18,... | collective-permute-start | bytes 98312 | tf_op jit(solution)/shard_map/while/body/eval_jaxpr/ppermute | solution.py:15
  95.4 1.9 collective-permute-start.2
  97.4 9.5 %collective-permute-done.2 = f32[1,8,64,256]{3,2,1,0:T(8,128)S(1)} collective-permute-done((f32[1,8,64,256]{3,2,1,0:T(8,128)S(1)}, f32[1,8,64,256]{3,2,1,0:T(8,128)S(1)}, u32[]{:S(2)}, u32[]{:S(2)}) %collective-permute-start.2) | collective-permute-done | bytes 524320 | tf_op jit(solution)/shard_map/while/body/eval_jaxpr/ppermute | solution.py:27
  108.3 4.5 %collective-permute-start.1 = (bf16[1,1,64,256]{3,2,1,0:T(8,128)(2,1)S(1)}, bf16[1,1,64,256]{3,2,1,0:T(8,128)(2,1)S(1)}, u32[]{:S(2)}, u32[]{:S(2)}) collective-permute-start(bf16[1,1,64,256]{3,2,1,0:T(8,128)(2,1)S(1)} %get-tuple-element.234), channel_id=1, source_target_pairs={{0,1},{2,3},{4,5},{6,7},{8,9},{10,11},{12,13},{14,15},{16,17},{18,... | collective-permute-start | bytes 98312 | tf_op jit(solution)/shard_map/while/body/eval_jaxpr/ppermute | solution.py:15
  115.3 1.9 collective-permute-start.2
  117.2 9.5 %collective-permute-done.2 = f32[1,8,64,256]{3,2,1,0:T(8,128)S(1)} collective-permute-done((f32[1,8,64,256]{3,2,1,0:T(8,128)S(1)}, f32[1,8,64,256]{3,2,1,0:T(8,128)S(1)}, u32[]{:S(2)}, u32[]{:S(2)}) %collective-permute-start.2) | collective-permute-done | bytes 524320 | tf_op jit(solution)/shard_map/while/body/eval_jaxpr/ppermute | solution.py:27
  128.2 4.5 %collective-permute-start.1 = (bf16[1,1,64,256]{3,2,1,0:T(8,128)(2,1)S(1)}, bf16[1,1,64,256]{3,2,1,0:T(8,128)(2,1)S(1)}, u32[]{:S(2)}, u32[]{:S(2)}) collective-permute-start(bf16[1,1,64,256]{3,2,1,0:T(8,128)(2,1)S(1)} %get-tuple-element.234), channel_id=1, source_target_pairs={{0,1},{2,3},{4,5},{6,7},{8,9},{10,11},{12,13},{14,15},{16,17},{18,... | collective-permute-start | bytes 98312 | tf_op jit(solution)/shard_map/while/body/eval_jaxpr/ppermute | solution.py:15
  137.1 9.5 %collective-permute-done.2 = f32[1,8,64,256]{3,2,1,0:T(8,128)S(1)} collective-permute-done((f32[1,8,64,256]{3,2,1,0:T(8,128)S(1)}, f32[1,8,64,256]{3,2,1,0:T(8,128)S(1)}, u32[]{:S(2)}, u32[]{:S(2)}) %collective-permute-start.2) | collective-permute-done | bytes 524320 | tf_op jit(solution)/shard_map/while/body/eval_jaxpr/ppermute | solution.py:27
  148.1 4.5 %collective-permute-start.1 = (bf16[1,1,64,256]{3,2,1,0:T(8,128)(2,1)S(1)}, bf16[1,1,64,256]{3,2,1,0:T(8,128)(2,1)S(1)}, u32[]{:S(2)}, u32[]{:S(2)}) collective-permute-start(bf16[1,1,64,256]{3,2,1,0:T(8,128)(2,1)S(1)} %get-tuple-element.234), channel_id=1, source_target_pairs={{0,1},{2,3},{4,5},{6,7},{8,9},{10,11},{12,13},{14,15},{16,17},{18,... | collective-permute-start | bytes 98312 | tf_op jit(solution)/shard_map/while/body/eval_jaxpr/ppermute | solution.py:15
  157.0 9.5 %collective-permute-done.2 = f32[1,8,64,256]{3,2,1,0:T(8,128)S(1)} collective-permute-done((f32[1,8,64,256]{3,2,1,0:T(8,128)S(1)}, f32[1,8,64,256]{3,2,1,0:T(8,128)S(1)}, u32[]{:S(2)}, u32[]{:S(2)}) %collective-permute-start.2) | collective-permute-done | bytes 524320 | tf_op jit(solution)/shard_map/while/body/eval_jaxpr/ppermute | solution.py:27
  167.9 4.5 %collective-permute-start.1 = (bf16[1,1,64,256]{3,2,1,0:T(8,128)(2,1)S(1)}, bf16[1,1,64,256]{3,2,1,0:T(8,128)(2,1)S(1)}, u32[]{:S(2)}, u32[]{:S(2)}) collective-permute-start(bf16[1,1,64,256]{3,2,1,0:T(8,128)(2,1)S(1)} %get-tuple-element.234), channel_id=1, source_target_pairs={{0,1},{2,3},{4,5},{6,7},{8,9},{10,11},{12,13},{14,15},{16,17},{18,... | collective-permute-start | bytes 98312 | tf_op jit(solution)/shard_map/while/body/eval_jaxpr/ppermute | solution.py:15
  174.9 1.9 collective-permute-start.2
  176.9 9.5 %collective-permute-done.2 = f32[1,8,64,256]{3,2,1,0:T(8,128)S(1)} collective-permute-done((f32[1,8,64,256]{3,2,1,0:T(8,128)S(1)}, f32[1,8,64,256]{3,2,1,0:T(8,128)S(1)}, u32[]{:S(2)}, u32[]{:S(2)}) %collective-permute-start.2) | collective-permute-done | bytes 524320 | tf_op jit(solution)/shard_map/while/body/eval_jaxpr/ppermute | solution.py:27
  187.8 4.5 %collective-permute-start.1 = (bf16[1,1,64,256]{3,2,1,0:T(8,128)(2,1)S(1)}, bf16[1,1,64,256]{3,2,1,0:T(8,128)(2,1)S(1)}, u32[]{:S(2)}, u32[]{:S(2)}) collective-permute-start(bf16[1,1,64,256]{3,2,1,0:T(8,128)(2,1)S(1)} %get-tuple-element.234), channel_id=1, source_target_pairs={{0,1},{2,3},{4,5},{6,7},{8,9},{10,11},{12,13},{14,15},{16,17},{18,... | collective-permute-start | bytes 98312 | tf_op jit(solution)/shard_map/while/body/eval_jaxpr/ppermute | solution.py:15
  196.7 9.5 %collective-permute-done.2 = f32[1,8,64,256]{3,2,1,0:T(8,128)S(1)} collective-permute-done((f32[1,8,64,256]{3,2,1,0:T(8,128)S(1)}, f32[1,8,64,256]{3,2,1,0:T(8,128)S(1)}, u32[]{:S(2)}, u32[]{:S(2)}) %collective-permute-start.2) | collective-permute-done | bytes 524320 | tf_op jit(solution)/shard_map/while/body/eval_jaxpr/ppermute | solution.py:27
  207.7 4.5 %collective-permute-start.1 = (bf16[1,1,64,256]{3,2,1,0:T(8,128)(2,1)S(1)}, bf16[1,1,64,256]{3,2,1,0:T(8,128)(2,1)S(1)}, u32[]{:S(2)}, u32[]{:S(2)}) collective-permute-start(bf16[1,1,64,256]{3,2,1,0:T(8,128)(2,1)S(1)} %get-tuple-element.234), channel_id=1, source_target_pairs={{0,1},{2,3},{4,5},{6,7},{8,9},{10,11},{12,13},{14,15},{16,17},{18,... | collective-permute-start | bytes 98312 | tf_op jit(solution)/shard_map/while/body/eval_jaxpr/ppermute | solution.py:15
  216.6 9.5 %collective-permute-done.2 = f32[1,8,64,256]{3,2,1,0:T(8,128)S(1)} collective-permute-done((f32[1,8,64,256]{3,2,1,0:T(8,128)S(1)}, f32[1,8,64,256]{3,2,1,0:T(8,128)S(1)}, u32[]{:S(2)}, u32[]{:S(2)}) %collective-permute-start.2) | collective-permute-done | bytes 524320 | tf_op jit(solution)/shard_map/while/body/eval_jaxpr/ppermute | solution.py:27
  227.5 4.5 %collective-permute-start.1 = (bf16[1,1,64,256]{3,2,1,0:T(8,128)(2,1)S(1)}, bf16[1,1,64,256]{3,2,1,0:T(8,128)(2,1)S(1)}, u32[]{:S(2)}, u32[]{:S(2)}) collective-permute-start(bf16[1,1,64,256]{3,2,1,0:T(8,128)(2,1)S(1)} %get-tuple-element.234), channel_id=1, source_target_pairs={{0,1},{2,3},{4,5},{6,7},{8,9},{10,11},{12,13},{14,15},{16,17},{18,... | collective-permute-start | bytes 98312 | tf_op jit(solution)/shard_map/while/body/eval_jaxpr/ppermute | solution.py:15
  234.5 1.9 collective-permute-start.2
  236.5 9.5 %collective-permute-done.2 = f32[1,8,64,256]{3,2,1,0:T(8,128)S(1)} collective-permute-done((f32[1,8,64,256]{3,2,1,0:T(8,128)S(1)}, f32[1,8,64,256]{3,2,1,0:T(8,128)S(1)}, u32[]{:S(2)}, u32[]{:S(2)}) %collective-permute-start.2) | collective-permute-done | bytes 524320 | tf_op jit(solution)/shard_map/while/body/eval_jaxpr/ppermute | solution.py:27
  247.4 4.5 %collective-permute-start.1 = (bf16[1,1,64,256]{3,2,1,0:T(8,128)(2,1)S(1)}, bf16[1,1,64,256]{3,2,1,0:T(8,128)(2,1)S(1)}, u32[]{:S(2)}, u32[]{:S(2)}) collective-permute-start(bf16[1,1,64,256]{3,2,1,0:T(8,128)(2,1)S(1)} %get-tuple-element.234), channel_id=1, source_target_pairs={{0,1},{2,3},{4,5},{6,7},{8,9},{10,11},{12,13},{14,15},{16,17},{18,... | collective-permute-start | bytes 98312 | tf_op jit(solution)/shard_map/while/body/eval_jaxpr/ppermute | solution.py:15
  256.3 9.5 %collective-permute-done.2 = f32[1,8,64,256]{3,2,1,0:T(8,128)S(1)} collective-permute-done((f32[1,8,64,256]{3,2,1,0:T(8,128)S(1)}, f32[1,8,64,256]{3,2,1,0:T(8,128)S(1)}, u32[]{:S(2)}, u32[]{:S(2)}) %collective-permute-start.2) | collective-permute-done | bytes 524320 | tf_op jit(solution)/shard_map/while/body/eval_jaxpr/ppermute | solution.py:27
  267.3 4.5 %collective-permute-start.1 = (bf16[1,1,64,256]{3,2,1,0:T(8,128)(2,1)S(1)}, bf16[1,1,64,256]{3,2,1,0:T(8,128)(2,1)S(1)}, u32[]{:S(2)}, u32[]{:S(2)}) collective-permute-start(bf16[1,1,64,256]{3,2,1,0:T(8,128)(2,1)S(1)} %get-tuple-element.234), channel_id=1, source_target_pairs={{0,1},{2,3},{4,5},{6,7},{8,9},{10,11},{12,13},{14,15},{16,17},{18,... | collective-permute-start | bytes 98312 | tf_op jit(solution)/shard_map/while/body/eval_jaxpr/ppermute | solution.py:15
  273.5 2.7 conditional.2
  278.8 9.5 %collective-permute-done.2 = f32[1,8,64,256]{3,2,1,0:T(8,128)S(1)} collective-permute-done((f32[1,8,64,256]{3,2,1,0:T(8,128)S(1)}, f32[1,8,64,256]{3,2,1,0:T(8,128)S(1)}, u32[]{:S(2)}, u32[]{:S(2)}) %collective-permute-start.2) | collective-permute-done | bytes 524320 | tf_op jit(solution)/shard_map/while/body/eval_jaxpr/ppermute | solution.py:27
  289.8 4.5 %collective-permute-start.1 = (bf16[1,1,64,256]{3,2,1,0:T(8,128)(2,1)S(1)}, bf16[1,1,64,256]{3,2,1,0:T(8,128)(2,1)S(1)}, u32[]{:S(2)}, u32[]{:S(2)}) collective-permute-start(bf16[1,1,64,256]{3,2,1,0:T(8,128)(2,1)S(1)} %get-tuple-element.234), channel_id=1, source_target_pairs={{0,1},{2,3},{4,5},{6,7},{8,9},{10,11},{12,13},{14,15},{16,17},{18,... | collective-permute-start | bytes 98312 | tf_op jit(solution)/shard_map/while/body/eval_jaxpr/ppermute | solution.py:15
  296.7 1.9 collective-permute-start.2
  298.7 9.5 %collective-permute-done.2 = f32[1,8,64,256]{3,2,1,0:T(8,128)S(1)} collective-permute-done((f32[1,8,64,256]{3,2,1,0:T(8,128)S(1)}, f32[1,8,64,256]{3,2,1,0:T(8,128)S(1)}, u32[]{:S(2)}, u32[]{:S(2)}) %collective-permute-start.2) | collective-permute-done | bytes 524320 | tf_op jit(solution)/shard_map/while/body/eval_jaxpr/ppermute | solution.py:27
  309.6 4.5 %collective-permute-start.1 = (bf16[1,1,64,256]{3,2,1,0:T(8,128)(2,1)S(1)}, bf16[1,1,64,256]{3,2,1,0:T(8,128)(2,1)S(1)}, u32[]{:S(2)}, u32[]{:S(2)}) collective-permute-start(bf16[1,1,64,256]{3,2,1,0:T(8,128)(2,1)S(1)} %get-tuple-element.234), channel_id=1, source_target_pairs={{0,1},{2,3},{4,5},{6,7},{8,9},{10,11},{12,13},{14,15},{16,17},{18,... | collective-permute-start | bytes 98312 | tf_op jit(solution)/shard_map/while/body/eval_jaxpr/ppermute | solution.py:15
  318.6 9.5 %collective-permute-done.2 = f32[1,8,64,256]{3,2,1,0:T(8,128)S(1)} collective-permute-done((f32[1,8,64,256]{3,2,1,0:T(8,128)S(1)}, f32[1,8,64,256]{3,2,1,0:T(8,128)S(1)}, u32[]{:S(2)}, u32[]{:S(2)}) %collective-permute-start.2) | collective-permute-done | bytes 524320 | tf_op jit(solution)/shard_map/while/body/eval_jaxpr/ppermute | solution.py:27
  328.2 4.2 %collective-permute-start.5 = (f32[1,4,64,256]{3,2,1,0:T(8,128)S(1)}, f32[1,4,64,256]{3,2,1,0:T(8,128)S(1)}, u32[]{:S(2)}, u32[]{:S(2)}) collective-permute-start(f32[1,4,64,256]{3,2,1,0:T(8,128)S(1)} %get-tuple-element.166), channel_id=1, source_target_pairs={{0,1},{2,3},{4,5},{6,7},{8,9},{10,11},{12,13},{14,15},{16,17},{18,... | collective-permute-start | bytes 786440 | tf_op jit(solution)/shard_map/ppermute | solution.py:15
  333.9 2.4 collective-permute-done.5
  336.4 4.3 %collective-permute-done.6 = f32[1,4,64,256]{3,2,1,0:T(8,128)S(1)} collective-permute-done((f32[1,4,64,256]{3,2,1,0:T(8,128)S(1)}, f32[1,4,64,256]{3,2,1,0:T(8,128)S(1)}, u32[]{:S(2)}, u32[]{:S(2)}) %collective-permute-start.6) | collective-permute-done | bytes 262176 | tf_op jit(solution)/shard_map/ppermute | solution.py:17
  350.9 2.3 fusion.150
  (302 shorter events, 100.2 us)
Async XLA Ops:
  2.5 11.2 %collective-permute-start.3 = (f32[1,4,64,256]{3,2,1,0:T(8,128)}, f32[1,4,64,256]{3,2,1,0:T(8,128)S(1)}, u32[]{:S(2)}, u32[]{:S(2)}) collective-permute-start(f32[1,4,64,256]{3,2,1,0:T(8,128)} %get-tuple-element.167), channel_id=1, source_target_pairs={{0,1},{2,3},{4,5},{6,7},{8,9},{10,11},{12,13},{14,15},{16,17},{18,... | collective-permute-start | bytes 786440 | tf_op jit(solution)/shard_map/ppermute | solution.py:15
  5.9 9.9 %collective-permute-start.4 = (f32[1,4,64,256]{3,2,1,0:T(8,128)}, f32[1,4,64,256]{3,2,1,0:T(8,128)S(1)}, u32[]{:S(2)}, u32[]{:S(2)}) collective-permute-start(f32[1,4,64,256]{3,2,1,0:T(8,128)} %get-tuple-element.168), channel_id=1, source_target_pairs={{1,0},{3,2},{5,4},{7,6},{9,8},{11,10},{13,12},{15,14},{17,16},{19,... | collective-permute-start | bytes 786440 | tf_op jit(solution)/shard_map/ppermute | solution.py:17
  27.6 5.9 %collective-permute-start = (bf16[1,1,64,256]{3,2,1,0:T(8,128)(2,1)S(1)}, bf16[1,1,64,256]{3,2,1,0:T(8,128)(2,1)S(1)}, u32[]{:S(2)}, u32[]{:S(2)}) collective-permute-start(bf16[1,1,64,256]{3,2,1,0:T(8,128)(2,1)S(1)} %get-tuple-element.233), channel_id=1, source_target_pairs={{1,0},{3,2},{5,4},{7,6},{9,8},{11,10},{13,12},{15,14},{17,16},{19,... | collective-permute-start | bytes 98312 | tf_op jit(solution)/shard_map/while/body/eval_jaxpr/ppermute | solution.py:17
  28.9 6.1 %collective-permute-start.1 = (bf16[1,1,64,256]{3,2,1,0:T(8,128)(2,1)S(1)}, bf16[1,1,64,256]{3,2,1,0:T(8,128)(2,1)S(1)}, u32[]{:S(2)}, u32[]{:S(2)}) collective-permute-start(bf16[1,1,64,256]{3,2,1,0:T(8,128)(2,1)S(1)} %get-tuple-element.234), channel_id=1, source_target_pairs={{0,1},{2,3},{4,5},{6,7},{8,9},{10,11},{12,13},{14,15},{16,17},{18,... | collective-permute-start | bytes 98312 | tf_op jit(solution)/shard_map/while/body/eval_jaxpr/ppermute | solution.py:15
  35.8 11.4 %collective-permute-start.2 = (f32[1,8,64,256]{3,2,1,0:T(8,128)S(1)}, f32[1,8,64,256]{3,2,1,0:T(8,128)S(1)}, u32[]{:S(2)}, u32[]{:S(2)}) collective-permute-start(f32[1,8,64,256]{3,2,1,0:T(8,128)S(1)} %add_add_fusion.2), channel_id=1, source_target_pairs={{0,2},{2,4},{4,6},{6,8},{8,10},{10,12},{12,14},{14,16},{16,18},{18... | collective-permute-start | bytes 1572872 | tf_op jit(solution)/shard_map/while/body/eval_jaxpr/ppermute | solution.py:27
  47.4 5.9 %collective-permute-start = (bf16[1,1,64,256]{3,2,1,0:T(8,128)(2,1)S(1)}, bf16[1,1,64,256]{3,2,1,0:T(8,128)(2,1)S(1)}, u32[]{:S(2)}, u32[]{:S(2)}) collective-permute-start(bf16[1,1,64,256]{3,2,1,0:T(8,128)(2,1)S(1)} %get-tuple-element.233), channel_id=1, source_target_pairs={{1,0},{3,2},{5,4},{7,6},{9,8},{11,10},{13,12},{15,14},{17,16},{19,... | collective-permute-start | bytes 98312 | tf_op jit(solution)/shard_map/while/body/eval_jaxpr/ppermute | solution.py:17
  48.7 6.1 %collective-permute-start.1 = (bf16[1,1,64,256]{3,2,1,0:T(8,128)(2,1)S(1)}, bf16[1,1,64,256]{3,2,1,0:T(8,128)(2,1)S(1)}, u32[]{:S(2)}, u32[]{:S(2)}) collective-permute-start(bf16[1,1,64,256]{3,2,1,0:T(8,128)(2,1)S(1)} %get-tuple-element.234), channel_id=1, source_target_pairs={{0,1},{2,3},{4,5},{6,7},{8,9},{10,11},{12,13},{14,15},{16,17},{18,... | collective-permute-start | bytes 98312 | tf_op jit(solution)/shard_map/while/body/eval_jaxpr/ppermute | solution.py:15
  55.7 11.4 %collective-permute-start.2 = (f32[1,8,64,256]{3,2,1,0:T(8,128)S(1)}, f32[1,8,64,256]{3,2,1,0:T(8,128)S(1)}, u32[]{:S(2)}, u32[]{:S(2)}) collective-permute-start(f32[1,8,64,256]{3,2,1,0:T(8,128)S(1)} %add_add_fusion.2), channel_id=1, source_target_pairs={{0,2},{2,4},{4,6},{6,8},{8,10},{10,12},{12,14},{14,16},{16,18},{18... | collective-permute-start | bytes 1572872 | tf_op jit(solution)/shard_map/while/body/eval_jaxpr/ppermute | solution.py:27
  67.3 5.9 %collective-permute-start = (bf16[1,1,64,256]{3,2,1,0:T(8,128)(2,1)S(1)}, bf16[1,1,64,256]{3,2,1,0:T(8,128)(2,1)S(1)}, u32[]{:S(2)}, u32[]{:S(2)}) collective-permute-start(bf16[1,1,64,256]{3,2,1,0:T(8,128)(2,1)S(1)} %get-tuple-element.233), channel_id=1, source_target_pairs={{1,0},{3,2},{5,4},{7,6},{9,8},{11,10},{13,12},{15,14},{17,16},{19,... | collective-permute-start | bytes 98312 | tf_op jit(solution)/shard_map/while/body/eval_jaxpr/ppermute | solution.py:17
  68.6 6.1 %collective-permute-start.1 = (bf16[1,1,64,256]{3,2,1,0:T(8,128)(2,1)S(1)}, bf16[1,1,64,256]{3,2,1,0:T(8,128)(2,1)S(1)}, u32[]{:S(2)}, u32[]{:S(2)}) collective-permute-start(bf16[1,1,64,256]{3,2,1,0:T(8,128)(2,1)S(1)} %get-tuple-element.234), channel_id=1, source_target_pairs={{0,1},{2,3},{4,5},{6,7},{8,9},{10,11},{12,13},{14,15},{16,17},{18,... | collective-permute-start | bytes 98312 | tf_op jit(solution)/shard_map/while/body/eval_jaxpr/ppermute | solution.py:15
  75.6 11.4 %collective-permute-start.2 = (f32[1,8,64,256]{3,2,1,0:T(8,128)S(1)}, f32[1,8,64,256]{3,2,1,0:T(8,128)S(1)}, u32[]{:S(2)}, u32[]{:S(2)}) collective-permute-start(f32[1,8,64,256]{3,2,1,0:T(8,128)S(1)} %add_add_fusion.2), channel_id=1, source_target_pairs={{0,2},{2,4},{4,6},{6,8},{8,10},{10,12},{12,14},{14,16},{16,18},{18... | collective-permute-start | bytes 1572872 | tf_op jit(solution)/shard_map/while/body/eval_jaxpr/ppermute | solution.py:27
  87.2 5.9 %collective-permute-start = (bf16[1,1,64,256]{3,2,1,0:T(8,128)(2,1)S(1)}, bf16[1,1,64,256]{3,2,1,0:T(8,128)(2,1)S(1)}, u32[]{:S(2)}, u32[]{:S(2)}) collective-permute-start(bf16[1,1,64,256]{3,2,1,0:T(8,128)(2,1)S(1)} %get-tuple-element.233), channel_id=1, source_target_pairs={{1,0},{3,2},{5,4},{7,6},{9,8},{11,10},{13,12},{15,14},{17,16},{19,... | collective-permute-start | bytes 98312 | tf_op jit(solution)/shard_map/while/body/eval_jaxpr/ppermute | solution.py:17
  88.5 6.1 %collective-permute-start.1 = (bf16[1,1,64,256]{3,2,1,0:T(8,128)(2,1)S(1)}, bf16[1,1,64,256]{3,2,1,0:T(8,128)(2,1)S(1)}, u32[]{:S(2)}, u32[]{:S(2)}) collective-permute-start(bf16[1,1,64,256]{3,2,1,0:T(8,128)(2,1)S(1)} %get-tuple-element.234), channel_id=1, source_target_pairs={{0,1},{2,3},{4,5},{6,7},{8,9},{10,11},{12,13},{14,15},{16,17},{18,... | collective-permute-start | bytes 98312 | tf_op jit(solution)/shard_map/while/body/eval_jaxpr/ppermute | solution.py:15
  95.4 11.4 %collective-permute-start.2 = (f32[1,8,64,256]{3,2,1,0:T(8,128)S(1)}, f32[1,8,64,256]{3,2,1,0:T(8,128)S(1)}, u32[]{:S(2)}, u32[]{:S(2)}) collective-permute-start(f32[1,8,64,256]{3,2,1,0:T(8,128)S(1)} %add_add_fusion.2), channel_id=1, source_target_pairs={{0,2},{2,4},{4,6},{6,8},{8,10},{10,12},{12,14},{14,16},{16,18},{18... | collective-permute-start | bytes 1572872 | tf_op jit(solution)/shard_map/while/body/eval_jaxpr/ppermute | solution.py:27
  107.0 5.9 %collective-permute-start = (bf16[1,1,64,256]{3,2,1,0:T(8,128)(2,1)S(1)}, bf16[1,1,64,256]{3,2,1,0:T(8,128)(2,1)S(1)}, u32[]{:S(2)}, u32[]{:S(2)}) collective-permute-start(bf16[1,1,64,256]{3,2,1,0:T(8,128)(2,1)S(1)} %get-tuple-element.233), channel_id=1, source_target_pairs={{1,0},{3,2},{5,4},{7,6},{9,8},{11,10},{13,12},{15,14},{17,16},{19,... | collective-permute-start | bytes 98312 | tf_op jit(solution)/shard_map/while/body/eval_jaxpr/ppermute | solution.py:17
  108.3 6.1 %collective-permute-start.1 = (bf16[1,1,64,256]{3,2,1,0:T(8,128)(2,1)S(1)}, bf16[1,1,64,256]{3,2,1,0:T(8,128)(2,1)S(1)}, u32[]{:S(2)}, u32[]{:S(2)}) collective-permute-start(bf16[1,1,64,256]{3,2,1,0:T(8,128)(2,1)S(1)} %get-tuple-element.234), channel_id=1, source_target_pairs={{0,1},{2,3},{4,5},{6,7},{8,9},{10,11},{12,13},{14,15},{16,17},{18,... | collective-permute-start | bytes 98312 | tf_op jit(solution)/shard_map/while/body/eval_jaxpr/ppermute | solution.py:15
  115.3 11.4 %collective-permute-start.2 = (f32[1,8,64,256]{3,2,1,0:T(8,128)S(1)}, f32[1,8,64,256]{3,2,1,0:T(8,128)S(1)}, u32[]{:S(2)}, u32[]{:S(2)}) collective-permute-start(f32[1,8,64,256]{3,2,1,0:T(8,128)S(1)} %add_add_fusion.2), channel_id=1, source_target_pairs={{0,2},{2,4},{4,6},{6,8},{8,10},{10,12},{12,14},{14,16},{16,18},{18... | collective-permute-start | bytes 1572872 | tf_op jit(solution)/shard_map/while/body/eval_jaxpr/ppermute | solution.py:27
  126.9 5.9 %collective-permute-start = (bf16[1,1,64,256]{3,2,1,0:T(8,128)(2,1)S(1)}, bf16[1,1,64,256]{3,2,1,0:T(8,128)(2,1)S(1)}, u32[]{:S(2)}, u32[]{:S(2)}) collective-permute-start(bf16[1,1,64,256]{3,2,1,0:T(8,128)(2,1)S(1)} %get-tuple-element.233), channel_id=1, source_target_pairs={{1,0},{3,2},{5,4},{7,6},{9,8},{11,10},{13,12},{15,14},{17,16},{19,... | collective-permute-start | bytes 98312 | tf_op jit(solution)/shard_map/while/body/eval_jaxpr/ppermute | solution.py:17
  128.2 6.1 %collective-permute-start.1 = (bf16[1,1,64,256]{3,2,1,0:T(8,128)(2,1)S(1)}, bf16[1,1,64,256]{3,2,1,0:T(8,128)(2,1)S(1)}, u32[]{:S(2)}, u32[]{:S(2)}) collective-permute-start(bf16[1,1,64,256]{3,2,1,0:T(8,128)(2,1)S(1)} %get-tuple-element.234), channel_id=1, source_target_pairs={{0,1},{2,3},{4,5},{6,7},{8,9},{10,11},{12,13},{14,15},{16,17},{18,... | collective-permute-start | bytes 98312 | tf_op jit(solution)/shard_map/while/body/eval_jaxpr/ppermute | solution.py:15
  135.2 11.4 %collective-permute-start.2 = (f32[1,8,64,256]{3,2,1,0:T(8,128)S(1)}, f32[1,8,64,256]{3,2,1,0:T(8,128)S(1)}, u32[]{:S(2)}, u32[]{:S(2)}) collective-permute-start(f32[1,8,64,256]{3,2,1,0:T(8,128)S(1)} %add_add_fusion.2), channel_id=1, source_target_pairs={{0,2},{2,4},{4,6},{6,8},{8,10},{10,12},{12,14},{14,16},{16,18},{18... | collective-permute-start | bytes 1572872 | tf_op jit(solution)/shard_map/while/body/eval_jaxpr/ppermute | solution.py:27
  146.8 5.9 %collective-permute-start = (bf16[1,1,64,256]{3,2,1,0:T(8,128)(2,1)S(1)}, bf16[1,1,64,256]{3,2,1,0:T(8,128)(2,1)S(1)}, u32[]{:S(2)}, u32[]{:S(2)}) collective-permute-start(bf16[1,1,64,256]{3,2,1,0:T(8,128)(2,1)S(1)} %get-tuple-element.233), channel_id=1, source_target_pairs={{1,0},{3,2},{5,4},{7,6},{9,8},{11,10},{13,12},{15,14},{17,16},{19,... | collective-permute-start | bytes 98312 | tf_op jit(solution)/shard_map/while/body/eval_jaxpr/ppermute | solution.py:17
  148.1 6.1 %collective-permute-start.1 = (bf16[1,1,64,256]{3,2,1,0:T(8,128)(2,1)S(1)}, bf16[1,1,64,256]{3,2,1,0:T(8,128)(2,1)S(1)}, u32[]{:S(2)}, u32[]{:S(2)}) collective-permute-start(bf16[1,1,64,256]{3,2,1,0:T(8,128)(2,1)S(1)} %get-tuple-element.234), channel_id=1, source_target_pairs={{0,1},{2,3},{4,5},{6,7},{8,9},{10,11},{12,13},{14,15},{16,17},{18,... | collective-permute-start | bytes 98312 | tf_op jit(solution)/shard_map/while/body/eval_jaxpr/ppermute | solution.py:15
  155.0 11.4 %collective-permute-start.2 = (f32[1,8,64,256]{3,2,1,0:T(8,128)S(1)}, f32[1,8,64,256]{3,2,1,0:T(8,128)S(1)}, u32[]{:S(2)}, u32[]{:S(2)}) collective-permute-start(f32[1,8,64,256]{3,2,1,0:T(8,128)S(1)} %add_add_fusion.2), channel_id=1, source_target_pairs={{0,2},{2,4},{4,6},{6,8},{8,10},{10,12},{12,14},{14,16},{16,18},{18... | collective-permute-start | bytes 1572872 | tf_op jit(solution)/shard_map/while/body/eval_jaxpr/ppermute | solution.py:27
  166.6 5.9 %collective-permute-start = (bf16[1,1,64,256]{3,2,1,0:T(8,128)(2,1)S(1)}, bf16[1,1,64,256]{3,2,1,0:T(8,128)(2,1)S(1)}, u32[]{:S(2)}, u32[]{:S(2)}) collective-permute-start(bf16[1,1,64,256]{3,2,1,0:T(8,128)(2,1)S(1)} %get-tuple-element.233), channel_id=1, source_target_pairs={{1,0},{3,2},{5,4},{7,6},{9,8},{11,10},{13,12},{15,14},{17,16},{19,... | collective-permute-start | bytes 98312 | tf_op jit(solution)/shard_map/while/body/eval_jaxpr/ppermute | solution.py:17
  167.9 6.1 %collective-permute-start.1 = (bf16[1,1,64,256]{3,2,1,0:T(8,128)(2,1)S(1)}, bf16[1,1,64,256]{3,2,1,0:T(8,128)(2,1)S(1)}, u32[]{:S(2)}, u32[]{:S(2)}) collective-permute-start(bf16[1,1,64,256]{3,2,1,0:T(8,128)(2,1)S(1)} %get-tuple-element.234), channel_id=1, source_target_pairs={{0,1},{2,3},{4,5},{6,7},{8,9},{10,11},{12,13},{14,15},{16,17},{18,... | collective-permute-start | bytes 98312 | tf_op jit(solution)/shard_map/while/body/eval_jaxpr/ppermute | solution.py:15
  174.9 11.4 %collective-permute-start.2 = (f32[1,8,64,256]{3,2,1,0:T(8,128)S(1)}, f32[1,8,64,256]{3,2,1,0:T(8,128)S(1)}, u32[]{:S(2)}, u32[]{:S(2)}) collective-permute-start(f32[1,8,64,256]{3,2,1,0:T(8,128)S(1)} %add_add_fusion.2), channel_id=1, source_target_pairs={{0,2},{2,4},{4,6},{6,8},{8,10},{10,12},{12,14},{14,16},{16,18},{18... | collective-permute-start | bytes 1572872 | tf_op jit(solution)/shard_map/while/body/eval_jaxpr/ppermute | solution.py:27
  186.5 5.9 %collective-permute-start = (bf16[1,1,64,256]{3,2,1,0:T(8,128)(2,1)S(1)}, bf16[1,1,64,256]{3,2,1,0:T(8,128)(2,1)S(1)}, u32[]{:S(2)}, u32[]{:S(2)}) collective-permute-start(bf16[1,1,64,256]{3,2,1,0:T(8,128)(2,1)S(1)} %get-tuple-element.233), channel_id=1, source_target_pairs={{1,0},{3,2},{5,4},{7,6},{9,8},{11,10},{13,12},{15,14},{17,16},{19,... | collective-permute-start | bytes 98312 | tf_op jit(solution)/shard_map/while/body/eval_jaxpr/ppermute | solution.py:17
  187.8 6.1 %collective-permute-start.1 = (bf16[1,1,64,256]{3,2,1,0:T(8,128)(2,1)S(1)}, bf16[1,1,64,256]{3,2,1,0:T(8,128)(2,1)S(1)}, u32[]{:S(2)}, u32[]{:S(2)}) collective-permute-start(bf16[1,1,64,256]{3,2,1,0:T(8,128)(2,1)S(1)} %get-tuple-element.234), channel_id=1, source_target_pairs={{0,1},{2,3},{4,5},{6,7},{8,9},{10,11},{12,13},{14,15},{16,17},{18,... | collective-permute-start | bytes 98312 | tf_op jit(solution)/shard_map/while/body/eval_jaxpr/ppermute | solution.py:15
  194.8 11.4 %collective-permute-start.2 = (f32[1,8,64,256]{3,2,1,0:T(8,128)S(1)}, f32[1,8,64,256]{3,2,1,0:T(8,128)S(1)}, u32[]{:S(2)}, u32[]{:S(2)}) collective-permute-start(f32[1,8,64,256]{3,2,1,0:T(8,128)S(1)} %add_add_fusion.2), channel_id=1, source_target_pairs={{0,2},{2,4},{4,6},{6,8},{8,10},{10,12},{12,14},{14,16},{16,18},{18... | collective-permute-start | bytes 1572872 | tf_op jit(solution)/shard_map/while/body/eval_jaxpr/ppermute | solution.py:27
  206.4 5.9 %collective-permute-start = (bf16[1,1,64,256]{3,2,1,0:T(8,128)(2,1)S(1)}, bf16[1,1,64,256]{3,2,1,0:T(8,128)(2,1)S(1)}, u32[]{:S(2)}, u32[]{:S(2)}) collective-permute-start(bf16[1,1,64,256]{3,2,1,0:T(8,128)(2,1)S(1)} %get-tuple-element.233), channel_id=1, source_target_pairs={{1,0},{3,2},{5,4},{7,6},{9,8},{11,10},{13,12},{15,14},{17,16},{19,... | collective-permute-start | bytes 98312 | tf_op jit(solution)/shard_map/while/body/eval_jaxpr/ppermute | solution.py:17
  207.7 6.1 %collective-permute-start.1 = (bf16[1,1,64,256]{3,2,1,0:T(8,128)(2,1)S(1)}, bf16[1,1,64,256]{3,2,1,0:T(8,128)(2,1)S(1)}, u32[]{:S(2)}, u32[]{:S(2)}) collective-permute-start(bf16[1,1,64,256]{3,2,1,0:T(8,128)(2,1)S(1)} %get-tuple-element.234), channel_id=1, source_target_pairs={{0,1},{2,3},{4,5},{6,7},{8,9},{10,11},{12,13},{14,15},{16,17},{18,... | collective-permute-start | bytes 98312 | tf_op jit(solution)/shard_map/while/body/eval_jaxpr/ppermute | solution.py:15
  214.7 11.4 %collective-permute-start.2 = (f32[1,8,64,256]{3,2,1,0:T(8,128)S(1)}, f32[1,8,64,256]{3,2,1,0:T(8,128)S(1)}, u32[]{:S(2)}, u32[]{:S(2)}) collective-permute-start(f32[1,8,64,256]{3,2,1,0:T(8,128)S(1)} %add_add_fusion.2), channel_id=1, source_target_pairs={{0,2},{2,4},{4,6},{6,8},{8,10},{10,12},{12,14},{14,16},{16,18},{18... | collective-permute-start | bytes 1572872 | tf_op jit(solution)/shard_map/while/body/eval_jaxpr/ppermute | solution.py:27
  227.5 6.1 %collective-permute-start.1 = (bf16[1,1,64,256]{3,2,1,0:T(8,128)(2,1)S(1)}, bf16[1,1,64,256]{3,2,1,0:T(8,128)(2,1)S(1)}, u32[]{:S(2)}, u32[]{:S(2)}) collective-permute-start(bf16[1,1,64,256]{3,2,1,0:T(8,128)(2,1)S(1)} %get-tuple-element.234), channel_id=1, source_target_pairs={{0,1},{2,3},{4,5},{6,7},{8,9},{10,11},{12,13},{14,15},{16,17},{18,... | collective-permute-start | bytes 98312 | tf_op jit(solution)/shard_map/while/body/eval_jaxpr/ppermute | solution.py:15
  234.5 11.4 %collective-permute-start.2 = (f32[1,8,64,256]{3,2,1,0:T(8,128)S(1)}, f32[1,8,64,256]{3,2,1,0:T(8,128)S(1)}, u32[]{:S(2)}, u32[]{:S(2)}) collective-permute-start(f32[1,8,64,256]{3,2,1,0:T(8,128)S(1)} %add_add_fusion.2), channel_id=1, source_target_pairs={{0,2},{2,4},{4,6},{6,8},{8,10},{10,12},{12,14},{14,16},{16,18},{18... | collective-permute-start | bytes 1572872 | tf_op jit(solution)/shard_map/while/body/eval_jaxpr/ppermute | solution.py:27
  246.1 5.9 %collective-permute-start = (bf16[1,1,64,256]{3,2,1,0:T(8,128)(2,1)S(1)}, bf16[1,1,64,256]{3,2,1,0:T(8,128)(2,1)S(1)}, u32[]{:S(2)}, u32[]{:S(2)}) collective-permute-start(bf16[1,1,64,256]{3,2,1,0:T(8,128)(2,1)S(1)} %get-tuple-element.233), channel_id=1, source_target_pairs={{1,0},{3,2},{5,4},{7,6},{9,8},{11,10},{13,12},{15,14},{17,16},{19,... | collective-permute-start | bytes 98312 | tf_op jit(solution)/shard_map/while/body/eval_jaxpr/ppermute | solution.py:17
  247.4 6.1 %collective-permute-start.1 = (bf16[1,1,64,256]{3,2,1,0:T(8,128)(2,1)S(1)}, bf16[1,1,64,256]{3,2,1,0:T(8,128)(2,1)S(1)}, u32[]{:S(2)}, u32[]{:S(2)}) collective-permute-start(bf16[1,1,64,256]{3,2,1,0:T(8,128)(2,1)S(1)} %get-tuple-element.234), channel_id=1, source_target_pairs={{0,1},{2,3},{4,5},{6,7},{8,9},{10,11},{12,13},{14,15},{16,17},{18,... | collective-permute-start | bytes 98312 | tf_op jit(solution)/shard_map/while/body/eval_jaxpr/ppermute | solution.py:15
  254.4 11.4 %collective-permute-start.2 = (f32[1,8,64,256]{3,2,1,0:T(8,128)S(1)}, f32[1,8,64,256]{3,2,1,0:T(8,128)S(1)}, u32[]{:S(2)}, u32[]{:S(2)}) collective-permute-start(f32[1,8,64,256]{3,2,1,0:T(8,128)S(1)} %add_add_fusion.2), channel_id=1, source_target_pairs={{0,2},{2,4},{4,6},{6,8},{8,10},{10,12},{12,14},{14,16},{16,18},{18... | collective-permute-start | bytes 1572872 | tf_op jit(solution)/shard_map/while/body/eval_jaxpr/ppermute | solution.py:27
  266.0 5.9 %collective-permute-start = (bf16[1,1,64,256]{3,2,1,0:T(8,128)(2,1)S(1)}, bf16[1,1,64,256]{3,2,1,0:T(8,128)(2,1)S(1)}, u32[]{:S(2)}, u32[]{:S(2)}) collective-permute-start(bf16[1,1,64,256]{3,2,1,0:T(8,128)(2,1)S(1)} %get-tuple-element.233), channel_id=1, source_target_pairs={{1,0},{3,2},{5,4},{7,6},{9,8},{11,10},{13,12},{15,14},{17,16},{19,... | collective-permute-start | bytes 98312 | tf_op jit(solution)/shard_map/while/body/eval_jaxpr/ppermute | solution.py:17
  267.3 6.1 %collective-permute-start.1 = (bf16[1,1,64,256]{3,2,1,0:T(8,128)(2,1)S(1)}, bf16[1,1,64,256]{3,2,1,0:T(8,128)(2,1)S(1)}, u32[]{:S(2)}, u32[]{:S(2)}) collective-permute-start(bf16[1,1,64,256]{3,2,1,0:T(8,128)(2,1)S(1)} %get-tuple-element.234), channel_id=1, source_target_pairs={{0,1},{2,3},{4,5},{6,7},{8,9},{10,11},{12,13},{14,15},{16,17},{18,... | collective-permute-start | bytes 98312 | tf_op jit(solution)/shard_map/while/body/eval_jaxpr/ppermute | solution.py:15
  276.9 11.4 %collective-permute-start.2 = (f32[1,8,64,256]{3,2,1,0:T(8,128)S(1)}, f32[1,8,64,256]{3,2,1,0:T(8,128)S(1)}, u32[]{:S(2)}, u32[]{:S(2)}) collective-permute-start(f32[1,8,64,256]{3,2,1,0:T(8,128)S(1)} %add_add_fusion.2), channel_id=1, source_target_pairs={{0,2},{2,4},{4,6},{6,8},{8,10},{10,12},{12,14},{14,16},{16,18},{18... | collective-permute-start | bytes 1572872 | tf_op jit(solution)/shard_map/while/body/eval_jaxpr/ppermute | solution.py:27
  288.5 5.9 %collective-permute-start = (bf16[1,1,64,256]{3,2,1,0:T(8,128)(2,1)S(1)}, bf16[1,1,64,256]{3,2,1,0:T(8,128)(2,1)S(1)}, u32[]{:S(2)}, u32[]{:S(2)}) collective-permute-start(bf16[1,1,64,256]{3,2,1,0:T(8,128)(2,1)S(1)} %get-tuple-element.233), channel_id=1, source_target_pairs={{1,0},{3,2},{5,4},{7,6},{9,8},{11,10},{13,12},{15,14},{17,16},{19,... | collective-permute-start | bytes 98312 | tf_op jit(solution)/shard_map/while/body/eval_jaxpr/ppermute | solution.py:17
  289.8 6.1 %collective-permute-start.1 = (bf16[1,1,64,256]{3,2,1,0:T(8,128)(2,1)S(1)}, bf16[1,1,64,256]{3,2,1,0:T(8,128)(2,1)S(1)}, u32[]{:S(2)}, u32[]{:S(2)}) collective-permute-start(bf16[1,1,64,256]{3,2,1,0:T(8,128)(2,1)S(1)} %get-tuple-element.234), channel_id=1, source_target_pairs={{0,1},{2,3},{4,5},{6,7},{8,9},{10,11},{12,13},{14,15},{16,17},{18,... | collective-permute-start | bytes 98312 | tf_op jit(solution)/shard_map/while/body/eval_jaxpr/ppermute | solution.py:15
  296.7 11.4 %collective-permute-start.2 = (f32[1,8,64,256]{3,2,1,0:T(8,128)S(1)}, f32[1,8,64,256]{3,2,1,0:T(8,128)S(1)}, u32[]{:S(2)}, u32[]{:S(2)}) collective-permute-start(f32[1,8,64,256]{3,2,1,0:T(8,128)S(1)} %add_add_fusion.2), channel_id=1, source_target_pairs={{0,2},{2,4},{4,6},{6,8},{8,10},{10,12},{12,14},{14,16},{16,18},{18... | collective-permute-start | bytes 1572872 | tf_op jit(solution)/shard_map/while/body/eval_jaxpr/ppermute | solution.py:27
  308.3 5.9 %collective-permute-start = (bf16[1,1,64,256]{3,2,1,0:T(8,128)(2,1)S(1)}, bf16[1,1,64,256]{3,2,1,0:T(8,128)(2,1)S(1)}, u32[]{:S(2)}, u32[]{:S(2)}) collective-permute-start(bf16[1,1,64,256]{3,2,1,0:T(8,128)(2,1)S(1)} %get-tuple-element.233), channel_id=1, source_target_pairs={{1,0},{3,2},{5,4},{7,6},{9,8},{11,10},{13,12},{15,14},{17,16},{19,... | collective-permute-start | bytes 98312 | tf_op jit(solution)/shard_map/while/body/eval_jaxpr/ppermute | solution.py:17
  309.6 6.1 %collective-permute-start.1 = (bf16[1,1,64,256]{3,2,1,0:T(8,128)(2,1)S(1)}, bf16[1,1,64,256]{3,2,1,0:T(8,128)(2,1)S(1)}, u32[]{:S(2)}, u32[]{:S(2)}) collective-permute-start(bf16[1,1,64,256]{3,2,1,0:T(8,128)(2,1)S(1)} %get-tuple-element.234), channel_id=1, source_target_pairs={{0,1},{2,3},{4,5},{6,7},{8,9},{10,11},{12,13},{14,15},{16,17},{18,... | collective-permute-start | bytes 98312 | tf_op jit(solution)/shard_map/while/body/eval_jaxpr/ppermute | solution.py:15
  316.6 11.4 %collective-permute-start.2 = (f32[1,8,64,256]{3,2,1,0:T(8,128)S(1)}, f32[1,8,64,256]{3,2,1,0:T(8,128)S(1)}, u32[]{:S(2)}, u32[]{:S(2)}) collective-permute-start(f32[1,8,64,256]{3,2,1,0:T(8,128)S(1)} %add_add_fusion.2), channel_id=1, source_target_pairs={{0,2},{2,4},{4,6},{6,8},{8,10},{10,12},{12,14},{14,16},{16,18},{18... | collective-permute-start | bytes 1572872 | tf_op jit(solution)/shard_map/while/body/eval_jaxpr/ppermute | solution.py:27
  328.2 8.1 %collective-permute-start.5 = (f32[1,4,64,256]{3,2,1,0:T(8,128)S(1)}, f32[1,4,64,256]{3,2,1,0:T(8,128)S(1)}, u32[]{:S(2)}, u32[]{:S(2)}) collective-permute-start(f32[1,4,64,256]{3,2,1,0:T(8,128)S(1)} %get-tuple-element.166), channel_id=1, source_target_pairs={{0,1},{2,3},{4,5},{6,7},{8,9},{10,11},{12,13},{14,15},{16,17},{18,... | collective-permute-start | bytes 786440 | tf_op jit(solution)/shard_map/ppermute | solution.py:15
  332.5 8.3 %collective-permute-start.6 = (f32[1,4,64,256]{3,2,1,0:T(8,128)S(1)}, f32[1,4,64,256]{3,2,1,0:T(8,128)S(1)}, u32[]{:S(2)}, u32[]{:S(2)}) collective-permute-start(f32[1,4,64,256]{3,2,1,0:T(8,128)S(1)} %get-tuple-element.165), channel_id=1, source_target_pairs={{1,0},{3,2},{5,4},{7,6},{9,8},{11,10},{13,12},{15,14},{17,16},{19,... | collective-permute-start | bytes 786440 | tf_op jit(solution)/shard_map/ppermute | solution.py:17
  (20 other events, 104.3 us)
where the time goes:
time: 355 us; the launch traced here: 353 us
  waiting for transfers between devices  174 us (49%)
  starting transfers between devices  127 us (36%)
  local copies, waits for them, and re-layouts  18.6 us (5%)
  matrix products  15.4 us (4%)
  other arithmetic  14.8 us (4%)
    ppermute x15, waiting for transfers between devices, from_behind(): return lax.ppermute(array, axis, pairs)  142 us
    ppermute x17, starting transfers between devices, extended_2(): lax.ppermute(tail, axis, [(i, (i + 1) % count) for i in range(ends)])  75.8 us
    ppermute x15, starting transfers between devices, from_behind(): return lax.ppermute(array, axis, pairs)  28.8 us
    ppermute x17, waiting for transfers between devices, extended_2(): lax.ppermute(tail, axis, [(i, (i + 1) % count) for i in range(ends)])  25.8 us
    ppermute x17, starting transfers between devices, extended_2(): lax.ppermute(head, axis, [((i + 1) % count, i) for i in range(ends)])  22.1 us
    dot_general x9, matrix products, conv_rows(): jnp.dot(stacked, kernel.reshape(9 * channels, channels), preferred_elemen...  15.4 us
    add x15, other arithmetic, turn(): advanced = carried + coarse_step * slope_term + defect  10.8 us
    unnamed x105, local copies, waits for them, and re-layouts  8.9 us
  transfers between devices with their start and end apart: 49, of which 33 were waited for; matrix products, arithmetic and copies ran while one was open for 2% of the time, Pallas kernels for 0%

commit v1 on v0

v1 whole, which is shorter than its diff:
```python
import functools

import jax
import jax.numpy as jnp
from jax import lax
from jax.experimental import pallas as pl
from jax.experimental.pallas import tpu as pltpu
from jax.sharding import PartitionSpec as P

MESH = pl.DeviceIdType.MESH


def kernel(
    slabs,
    bands,
    start,
    weights,
    biases,
    steps,
    corrected,
    ends,
    cols,
    current,
    defect,
    advanced,
    inbox,
    halo,
    stage,
    row_send,
    row_recv,
    halo_send,
    halo_recv,
):
    rows, width, channels = start.shape
    layers = weights.shape[0]
    half = rows // 2
    slab = lax.axis_index("fine")
    band = lax.axis_index("coarse")
    total_step = steps[0]
    for layer in range(1, layers):
        total_step = total_step + steps[layer]

    def has_band(side):
        other = band + 2 * side - 1
        return (other >= 0) & (other < bands)

    barrier = pltpu.get_barrier_semaphore()
    around = [(i, j) for i in (-1, 0, 1) for j in (-1, 0, 1) if (i, j) != (0, 0)]
    for i, j in around:
        there = (slab + i >= 0) & (slab + i < slabs) & (band + j >= 0) & (band + j < bands)

        @pl.when(there)
        def _():
            pl.semaphore_signal(
                barrier, inc=1, device_id=(slab + i, band + j), device_id_type=MESH
            )

    def span(at, count):
        return 1 + jnp.where(at > 0, 1, 0) + jnp.where(at < count - 1, 1, 0)

    pl.semaphore_wait(barrier, span(slab, slabs) * span(band, bands) - 1)

    def widened(value):
        count = value.shape[0]
        column = lax.rem(lax.broadcasted_iota(jnp.int32, value.shape, 0), width)
        left = jnp.where(column == 0, 0.0, pltpu.roll(value, 1, 0))
        right = jnp.where(column == width - 1, 0.0, pltpu.roll(value, count - 1, 0))
        return jnp.concatenate([left, value, right], axis=-1).astype(jnp.bfloat16)

    def put(parity, place, value):
        count = value.shape[0] // width
        cols[parity, pl.ds(place, count)] = widened(value).reshape(count, width, 3 * channels)

    def slope(parity, first, count, layer):
        taps = [
            cols[parity, pl.ds(first + a, count)].reshape(count * width, 3 * channels)
            for a in range(3)
        ]
        product = jnp.dot(
            jnp.concatenate(taps, axis=-1), weights[layer], preferred_element_type=jnp.float32
        )
        return jnp.tanh(product + biases[pl.ds(layer, 1), :])

    def halo_copy(slot, side, ahead):
        return pltpu.make_async_remote_copy(
            src_ref=stage.at[slot, side],
            dst_ref=halo.at[slot, 1 - side],
            send_sem=halo_send.at[slot, side],
            recv_sem=halo_recv.at[slot, 1 - side],
            device_id=(slab + ahead, band + 2 * side - 1),
            device_id_type=MESH,
        )

    def send_halo(slot, side, value, ahead=0):
        @pl.when(has_band(side))
        def _():
            stage[slot, side] = value.astype(jnp.bfloat16)
            halo_copy(slot, side, ahead).start()

    def take_halo(slot, side, parity):
        @pl.when(has_band(side))
        def _():
            pltpu.make_async_remote_copy(
                src_ref=stage.at[slot, 1 - side],
                dst_ref=halo.at[slot, side],
                send_sem=halo_send.at[slot, 1 - side],
                recv_sem=halo_recv.at[slot, side],
                device_id=(slab, band + 2 * side - 1),
                device_id_type=MESH,
            ).wait_recv()
            put(parity, side * (rows + 1), halo[slot, side].astype(jnp.float32))

    def row_copy(row):
        return pltpu.make_async_remote_copy(
            src_ref=advanced.at[row],
            dst_ref=inbox.at[row],
            send_sem=row_send.at[row],
            recv_sem=row_recv.at[row],
            device_id=(slab + 1, band),
            device_id_type=MESH,
        )

    def layer_step(base, layer, relaxing):
        parity = lax.rem(layer, 2)

        def part(at, carry):
            side = lax.rem(at + band, 2)
            first = side * half
            take_halo(base + layer, side, parity)
            before = current[pl.ds(first, half)].reshape(half * width, channels)
            slope_term = slope(parity, first, half, layer)
            after = before + steps[layer] * slope_term
            current[pl.ds(first, half)] = after.reshape(half, width, channels)

            @pl.when(layer < layers - 1)
            def _():
                send_halo(base + layer + 1, side, current[side * (rows - 1)])
                put(1 - parity, first + 1, after)

            if relaxing:

                @pl.when(layer == 0)
                def _():
                    coarse = before + total_step * slope_term
                    defect[pl.ds(first, half)] = -coarse.reshape(half, width, channels)

                @pl.when(layer == layers - 1)
                def _():
                    defect[pl.ds(first, half)] += after.reshape(half, width, channels)

            return carry

        lax.fori_loop(0, 2, part, 0)

    for side in range(2):
        send_halo(0, side, start[side * (rows - 1)])

    @pl.when(band == 0)
    def _():
        cols[:, 0] = jnp.zeros((2, width, 3 * channels), jnp.bfloat16)

    @pl.when(band == bands - 1)
    def _():
        cols[:, rows + 1] = jnp.zeros((2, width, 3 * channels), jnp.bfloat16)

    def load(row, carry):
        current[row] = start[row]
        put(0, row + 1, start[row])
        return carry

    lax.fori_loop(0, rows, load, 0)

    def relax(layer, carry):
        layer_step(0, layer, True)
        return carry

    lax.fori_loop(0, layers, relax, 0)

    near = 1 - lax.rem(band, 2)
    far = 1 - near

    def place(at):
        return near * (rows - 1) + (1 - 2 * near) * at

    @pl.when(slab == 0)
    def _():
        def hand_on(at, carry):
            row = place(at)
            value = current[row]
            advanced[row] = value

            @pl.when(slab < slabs - 1)
            def _():
                row_copy(row).start()

                @pl.when(at == 0)
                def _():
                    send_halo(layers, near, value, 1)

                @pl.when(at == rows - 1)
                def _():
                    send_halo(layers, far, value, 1)

            return carry

        lax.fori_loop(0, rows, hand_on, 0)
        corrected[...] = start[...]
        ends[...] = current[...]

    @pl.when(slab > 0)
    def _():
        def take_row(row):
            row_copy(row).wait_recv()
            put(0, row + 1, inbox[row])

        take_row(place(0))
        take_halo(layers, near, 0)

        def chain(at, carry):
            row = place(at)

            @pl.when(at < rows - 1)
            def _():
                take_row(place(at + 1))

            @pl.when(at == rows - 1)
            def _():
                take_halo(layers, far, 0)

            slope_term = slope(0, row, 1, 0)
            value = inbox[row]
            following = value + total_step * slope_term + defect[row]

            @pl.when(slab < slabs - 1)
            def _():
                advanced[row] = following
                row_copy(row).start()

                @pl.when(at == 0)
                def _():
                    send_halo(layers, near, following, 1)

                @pl.when(at == rows - 1)
                def _():
                    send_halo(layers, far, following, 1)

            after = value + steps[0] * slope_term
            if layers > 1:

                @pl.when(at == 0)
                def _():
                    send_halo(layers + 1, near, after)

                @pl.when(at == rows - 1)
                def _():
                    send_halo(layers + 1, far, after)

            current[row] = after
            put(1, row + 1, after)
            corrected[row] = value
            return carry

        lax.fori_loop(0, rows, chain, 0)

        def finish(layer, carry):
            layer_step(layers, layer, False)
            return carry

        lax.fori_loop(1, layers, finish, 0)
        ends[...] = current[...]

    for side in range(2):

        @pl.when(has_band(side))
        def _():
            for slot in range(layers):
                halo_copy(slot, side, 0).wait_send()

            @pl.when(slab < slabs - 1)
            def _():
                halo_copy(layers, side, 1).wait_send()

            @pl.when(slab > 0)
            def _():
                for slot in range(layers + 1, 2 * layers):
                    halo_copy(slot, side, 0).wait_send()

    @pl.when(slab < slabs - 1)
    def _():
        for row in range(rows):
            row_copy(row).wait_send()


def local(start_states, weights, biases, step_sizes):
    rows, width, channels = start_states.shape[2:]
    layers = weights.shape[0]
    state = (rows, width, channels)
    slots = 2 * layers
    whole = pl.BlockSpec(memory_space=pltpu.VMEM)
    shape = jax.ShapeDtypeStruct(state, jnp.float32)
    corrected, ends = pl.pallas_call(
        functools.partial(kernel, lax.axis_size("fine"), lax.axis_size("coarse")),
        out_shape=(shape, shape),
        in_specs=[whole, whole, whole, pl.BlockSpec(memory_space=pltpu.SMEM)],
        out_specs=(whole, whole),
        scratch_shapes=[
            pltpu.VMEM((2, rows + 2, width, 3 * channels), jnp.bfloat16),
            pltpu.VMEM(state, jnp.float32),
            pltpu.VMEM(state, jnp.float32),
            pltpu.VMEM(state, jnp.float32),
            pltpu.VMEM(state, jnp.float32),
            pltpu.VMEM((slots, 2, width, channels), jnp.bfloat16),
            pltpu.VMEM((slots, 2, width, channels), jnp.bfloat16),
            pltpu.SemaphoreType.DMA((rows,)),
            pltpu.SemaphoreType.DMA((rows,)),
            pltpu.SemaphoreType.DMA((slots, 2)),
            pltpu.SemaphoreType.DMA((slots, 2)),
        ],
        compiler_params=pltpu.CompilerParams(
            collective_id=0, has_side_effects=True, vmem_limit_bytes=40 * 1024 * 1024
        ),
    )(
        start_states.reshape(state),
        weights.reshape(layers, 9 * channels, channels),
        biases,
        step_sizes,
    )
    return (corrected.reshape(start_states.shape), ends.reshape(start_states.shape))


def solution(mesh):
    in_specs = (
        P("fine", None, "coarse", None, None),
        P("fine", None, None, None),
        P("fine", None),
        P("fine"),
    )
    out_specs = (P("fine", None, "coarse", None, None), P("fine", None, "coarse", None, None))
    return jax.shard_map(local, mesh=mesh, in_specs=in_specs, out_specs=out_specs, check_vma=False)
```

time: 355 us -> 86.8 us (0.24)
  the two profiles are of different devices: /device:TPU:24 before, /device:TPU:27 now
where the time goes in v1:
time: 86.8 us; the launch traced here: 86.6 us
  Pallas kernels  79.6 us (92%)
  local copies, waits for them, and re-layouts  6.3 us (7%)
    pallas_call x1, Pallas kernels, local(): pl.pallas_call(functools.partial(kernel, lax.axis_size('fine'), lax.axis_...  79.6 us
    unnamed x10, local copies, waits for them, and re-layouts  6.3 us

profile of v1, /device:TPU:27, one launch (start us, length us, event | category | flops | bytes accessed | tf_op | source)
XLA Modules:
  0.0 86.6 jit_solution(3957089186258036591)
XLA Ops:
  0.6 0.0 copy-start
  0.6 2.3 %copy-done = bf16[4,9,256,256]{3,2,1,0:T(8,128)(2,1)S(1)} copy-done((bf16[4,9,256,256]{3,2,1,0:T(8,128)(2,1)S(1)}, bf16[4,9,256,256]{3,2,1,0:T(8,128)(2,1)}, u32[]{:S(2)}) %copy-start) | copy-done | bytes 4718616
  3.0 0.0 copy-start.1
  3.0 1.0 %copy-done.1 = f32[1,1,8,64,256]{4,3,2,1,0:T(8,128)S(1)} copy-done((f32[1,1,8,64,256]{4,3,2,1,0:T(8,128)S(1)}, f32[1,1,8,64,256]{4,3,2,1,0:T(8,128)}, u32[]{:S(2)}) %copy-start.1) | copy-done | bytes 524312
  4.0 0.0 copy-start.2
  4.0 0.7 copy-done.2
  4.7 0.0 copy-start.3
  4.7 0.7 copy-done.3
  5.4 79.6 %shard_map.59 = (f32[8,64,256]{2,1,0:T(8,128)S(1)}, f32[8,64,256]{2,1,0:T(8,128)S(1)}) custom-call(f32[8,64,256]{2,1,0:T(8,128)S(1)} %bitcast.5, bf16[4,2304,256]{2,1,0:T(8,128)(2,1)S(1)} %bitcast.4, f32[4,256]{1,0:T(4,128)S(1)} %copy-done.2, f32[4]{0:T(128)S(1)} %copy-done.3), custom_call_target="tpu_custom_call" | custom-call | tf_op jit(solution)/shard_map/pallas_call | solution.py:301
  85.0 0.8 copy.8
  85.8 0.8 copy.9
Async XLA Ops:
  0.6 2.3 %copy-start = (bf16[4,9,256,256]{3,2,1,0:T(8,128)(2,1)S(1)}, bf16[4,9,256,256]{3,2,1,0:T(8,128)(2,1)}, u32[]{:S(2)}) copy-start(bf16[4,9,256,256]{3,2,1,0:T(8,128)(2,1)} %param.5) | copy-start | bytes 14155780
  3.0 1.0 %copy-start.1 = (f32[1,1,8,64,256]{4,3,2,1,0:T(8,128)S(1)}, f32[1,1,8,64,256]{4,3,2,1,0:T(8,128)}, u32[]{:S(2)}) copy-start(f32[1,1,8,64,256]{4,3,2,1,0:T(8,128)} %param.4) | copy-start | bytes 1572868
  4.0 0.7 copy-start.2
  4.7 0.7 copy-start.3

commit v2 on v1

--- a/solution.py
+++ b/solution.py
@@ -14,7 +14,7 @@
     slabs,
     bands,
     start,
-    weights,
+    stored_weights,
     biases,
     steps,
     corrected,
@@ -30,9 +30,23 @@
     row_recv,
     halo_send,
     halo_recv,
+    weights,
+    load_sem,
 ):
     rows, width, channels = start.shape
     layers = weights.shape[0]
+    window = min(2, rows)
+    state_load = pltpu.make_async_copy(start, current, load_sem.at[layers])
+    state_load.start()
+
+    def weight_load(layer):
+        return pltpu.make_async_copy(
+            stored_weights.at[layer], weights.at[layer], load_sem.at[layer]
+        )
+
+    for layer in range(layers):
+        weight_load(layer).start()
+
     half = rows // 2
     slab = lax.axis_index("fine")
     band = lax.axis_index("coarse")
@@ -152,8 +166,15 @@
 
         lax.fori_loop(0, 2, part, 0)
 
+    first_load = pltpu.make_async_copy(start, corrected, load_sem.at[layers + 1])
+
+    @pl.when(slab == 0)
+    def _():
+        first_load.start()
+
+    state_load.wait()
     for side in range(2):
-        send_halo(0, side, start[side * (rows - 1)])
+        send_halo(0, side, current[side * (rows - 1)])
 
     @pl.when(band == 0)
     def _():
@@ -164,13 +185,13 @@
         cols[:, rows + 1] = jnp.zeros((2, width, 3 * channels), jnp.bfloat16)
 
     def load(row, carry):
-        current[row] = start[row]
-        put(0, row + 1, start[row])
+        put(0, row + 1, current[row])
         return carry
 
     lax.fori_loop(0, rows, load, 0)
 
     def relax(layer, carry):
+        weight_load(layer).wait()
         layer_step(0, layer, True)
         return carry
 
@@ -181,6 +202,13 @@
 
     def place(at):
         return near * (rows - 1) + (1 - 2 * near) * at
+
+    def send_row(at):
+        @pl.when(at >= window)
+        def _():
+            row_copy(place(at - window)).wait_send()
+
+        row_copy(place(at)).start()
 
     @pl.when(slab == 0)
     def _():
@@ -191,7 +219,7 @@
 
             @pl.when(slab < slabs - 1)
             def _():
-                row_copy(row).start()
+                send_row(at)
 
                 @pl.when(at == 0)
                 def _():
@@ -204,7 +232,7 @@
             return carry
 
         lax.fori_loop(0, rows, hand_on, 0)
-        corrected[...] = start[...]
+        first_load.wait()
         ends[...] = current[...]
 
     @pl.when(slab > 0)
@@ -234,7 +262,7 @@
             @pl.when(slab < slabs - 1)
             def _():
                 advanced[row] = following
-                row_copy(row).start()
+                send_row(at)
 
                 @pl.when(at == 0)
                 def _():
@@ -287,8 +315,8 @@
 
     @pl.when(slab < slabs - 1)
     def _():
-        for row in range(rows):
-            row_copy(row).wait_send()
+        for at in range(rows - window, rows):
+            row_copy(place(at)).wait_send()
 
 
 def local(start_states, weights, biases, step_sizes):
@@ -296,12 +324,13 @@
     layers = weights.shape[0]
     state = (rows, width, channels)
     slots = 2 * layers
+    anywhere = pl.BlockSpec(memory_space=pl.ANY)
     whole = pl.BlockSpec(memory_space=pltpu.VMEM)
     shape = jax.ShapeDtypeStruct(state, jnp.float32)
     corrected, ends = pl.pallas_call(
         functools.partial(kernel, lax.axis_size("fine"), lax.axis_size("coarse")),
         out_shape=(shape, shape),
-        in_specs=[whole, whole, whole, pl.BlockSpec(memory_space=pltpu.SMEM)],
+        in_specs=[anywhere, anywhere, whole, pl.BlockSpec(memory_space=pltpu.SMEM)],
         out_specs=(whole, whole),
         scratch_shapes=[
             pltpu.VMEM((2, rows + 2, width, 3 * channels), jnp.bfloat16),
@@ -315,9 +344,11 @@
             pltpu.SemaphoreType.DMA((rows,)),
             pltpu.SemaphoreType.DMA((slots, 2)),
             pltpu.SemaphoreType.DMA((slots, 2)),
+            pltpu.VMEM((layers, 9 * channels, channels), jnp.bfloat16),
+            pltpu.SemaphoreType.DMA((layers + 2,)),
         ],
         compiler_params=pltpu.CompilerParams(
-            collective_id=0, has_side_effects=True, vmem_limit_bytes=40 * 1024 * 1024
+            collective_id=0, has_side_effects=True, vmem_limit_bytes=56 * 1024 * 1024
         ),
     )(
         start_states.reshape(state),

time: 86.8 us -> 86.1 us (level)
  local copies, waits for them, and re-layouts: 6.3 us -> 3.74 us
  Pallas kernels: 79.6 us -> 81.5 us
    unnamed x10 -> x2, local copies, waits for them, and re-layouts: 6.3 us -> 3.74 us
    pallas_call x1, Pallas kernels: 79.6 us -> 81.5 us  [local(): pl.pallas_call(functools.partial(kernel, lax.axis_size('fine'), lax.axis_...]
where the time goes in v2:
time: 86.1 us; the launch traced here: 85.9 us
  Pallas kernels  81.5 us (95%)
  local copies, waits for them, and re-layouts  3.74 us (4%)
    pallas_call x1, Pallas kernels, local(): pl.pallas_call(functools.partial(kernel, lax.axis_size('fine'), lax.axis_...  81.5 us
    unnamed x2, local copies, waits for them, and re-layouts  3.74 us

profile of v2, /device:TPU:27, one launch (start us, length us, event | category | flops | bytes accessed | tf_op | source)
XLA Modules:
  0.0 85.9 jit_solution(9160172204676795630)
XLA Ops:
  0.6 81.5 %shard_map.59 = (f32[8,64,256]{2,1,0:T(8,128)}, f32[8,64,256]{2,1,0:T(8,128)}) custom-call(f32[8,64,256]{2,1,0:T(8,128)} %bitcast.5, bf16[4,2304,256]{2,1,0:T(8,128)(2,1)} %bitcast.4, f32[4,256]{1,0:T(4,128)} %biases.1, f32[4]{0:T(128)} %steps.1), custom_call_target="tpu_custom_call" | custom-call | tf_op jit(solution)/shard_map/pallas_call | solution.py:330
  82.2 1.9 %copy.8 = f32[1,1,8,64,256]{4,3,2,1,0:T(8,128)} copy(f32[1,1,8,64,256]{4,3,2,1,0:T(8,128)} %bitcast.7) | data formatting | bytes 1048576
  84.0 1.9 %copy.9 = f32[1,1,8,64,256]{4,3,2,1,0:T(8,128)} copy(f32[1,1,8,64,256]{4,3,2,1,0:T(8,128)} %bitcast.6) | data formatting | bytes 1048576

commit v3 on v2

v3 whole, which is shorter than its diff:
```python
import functools

import jax
import jax.numpy as jnp
from jax import lax
from jax.experimental import pallas as pl
from jax.experimental.pallas import tpu as pltpu
from jax.sharding import PartitionSpec as P

MESH = pl.DeviceIdType.MESH


def kernel(
    slabs,
    bands,
    start,
    stored_weights,
    biases,
    steps,
    corrected,
    ends,
    cols,
    current,
    defect,
    advanced,
    inbox,
    narrow,
    narrow_inbox,
    edge,
    halo,
    row_send,
    row_recv,
    halo_send,
    halo_recv,
    weights,
    load_sem,
):
    rows, width, channels = start.shape
    layers = weights.shape[0]
    own = pl.ds(layers, rows)
    state_load = pltpu.make_async_copy(start, current.at[own], load_sem.at[layers])
    state_load.start()

    def weight_load(layer):
        return pltpu.make_async_copy(
            stored_weights.at[layer], weights.at[layer], load_sem.at[layer]
        )

    for layer in range(layers):
        weight_load(layer).start()

    slab = lax.axis_index("fine")
    band = lax.axis_index("coarse")
    total_step = steps[0]
    for layer in range(1, layers):
        total_step = total_step + steps[layer]

    def has_band(side):
        other = band + 2 * side - 1
        return (other >= 0) & (other < bands)

    barrier = pltpu.get_barrier_semaphore()
    around = [(i, j) for i in (-1, 0, 1) for j in (-1, 0, 1) if (i, j) != (0, 0)]
    for i, j in around:
        there = (slab + i >= 0) & (slab + i < slabs) & (band + j >= 0) & (band + j < bands)

        @pl.when(there)
        def _():
            pl.semaphore_signal(
                barrier, inc=1, device_id=(slab + i, band + j), device_id_type=MESH
            )

    def span(at, count):
        return 1 + jnp.where(at > 0, 1, 0) + jnp.where(at < count - 1, 1, 0)

    pl.semaphore_wait(barrier, span(slab, slabs) * span(band, bands) - 1)

    def widened(value):
        count = value.shape[0]
        column = lax.rem(lax.broadcasted_iota(jnp.int32, value.shape, 0), width)
        left = jnp.where(column == 0, 0.0, pltpu.roll(value, 1, 0))
        right = jnp.where(column == width - 1, 0.0, pltpu.roll(value, count - 1, 0))
        return jnp.concatenate([left, value, right], axis=-1).astype(jnp.bfloat16)

    def put(parity, place, value):
        count = value.shape[0] // width
        cols[parity, pl.ds(place, count)] = widened(value).reshape(count, width, 3 * channels)

    def slope(parity, first, count, layer):
        taps = [
            cols[parity, pl.ds(first + a, count)].reshape(count * width, 3 * channels)
            for a in range(3)
        ]
        product = jnp.dot(
            jnp.concatenate(taps, axis=-1), weights[layer], preferred_element_type=jnp.float32
        )
        return jnp.tanh(product + biases[pl.ds(layer, 1), :])

    first_load = pltpu.make_async_copy(start, corrected, load_sem.at[layers + 1])

    @pl.when(slab == 0)
    def _():
        first_load.start()

    def margin_copy(side):
        return pltpu.make_async_remote_copy(
            src_ref=edge.at[side],
            dst_ref=halo.at[0, 1 - side],
            send_sem=halo_send.at[0, side, 0],
            recv_sem=halo_recv.at[0, 1 - side, 0],
            device_id=(slab, band + 2 * side - 1),
            device_id_type=MESH,
        )

    def cross_copy(side, at):
        return pltpu.make_async_remote_copy(
            src_ref=narrow.at[side * (rows - layers) + at],
            dst_ref=halo.at[1, 1 - side, at],
            send_sem=halo_send.at[1, side, at],
            recv_sem=halo_recv.at[1, 1 - side, at],
            device_id=(slab + 1, band + 2 * side - 1),
            device_id_type=MESH,
        )

    def wide_copy(row):
        return pltpu.make_async_remote_copy(
            src_ref=advanced.at[row],
            dst_ref=inbox.at[row],
            send_sem=row_send.at[row],
            recv_sem=row_recv.at[row],
            device_id=(slab + 1, band),
            device_id_type=MESH,
        )

    def narrow_copy(row):
        return pltpu.make_async_remote_copy(
            src_ref=narrow.at[row],
            dst_ref=narrow_inbox.at[row],
            send_sem=row_send.at[row],
            recv_sem=row_recv.at[row],
            device_id=(slab + 1, band),
            device_id_type=MESH,
        )

    odd = lax.rem(slab, 2)

    def send_row(row, value):
        narrow[row] = value.astype(jnp.bfloat16)

        @pl.when(odd == 1)
        def _():
            narrow_copy(row).start()

        @pl.when(odd == 0)
        def _():
            advanced[row] = value
            wide_copy(row).start()

        for side in range(2):
            at = row - side * (rows - layers)

            @pl.when(has_band(side) & (at >= 0) & (at < layers))
            def _():
                cross_copy(side, at).start()

    def set_margin(phase, side, at):
        value = halo[phase, side, at].astype(jnp.float32)
        spot = side * (layers + rows) + at
        current[spot] = value
        put(0, spot, value)

    def take_cross(side, at):
        @pl.when(has_band(side))
        def _():
            pltpu.make_async_remote_copy(
                src_ref=narrow.at[at],
                dst_ref=halo.at[1, side, at],
                send_sem=halo_send.at[1, 1 - side, at],
                recv_sem=halo_recv.at[1, side, at],
                device_id=(slab, band + 2 * side - 1),
                device_id_type=MESH,
            ).wait_recv()
            set_margin(1, side, at)

    def layer_step(layer, relaxing):
        margin = layers - 1 - layer
        parity = layer % 2
        if bands == 1:
            first, count = layers, rows
        elif bands == 2:
            first, count = layers - margin * band, rows + margin
        else:
            first, count = layers - margin, rows + 2 * margin
        before = current[pl.ds(first, count)].reshape(count * width, channels)
        slope_term = slope(parity, first - 1, count, layer)
        after = before + steps[layer] * slope_term
        if bands > 2:
            spot = first + lax.broadcasted_iota(jnp.int32, after.shape, 0) // width
            outside = ((band == 0) & (spot < layers)) | (
                (band == bands - 1) & (spot >= layers + rows)
            )
            after = jnp.where(outside, 0.0, after)
        current[pl.ds(first, count)] = after.reshape(count, width, channels)
        if layer < layers - 1:
            put(1 - parity, first, after)
        if relaxing and layer == 0:
            coarse = (before + total_step * slope_term).reshape(count, width, channels)
            if bands == 2:

                @pl.when(band == 0)
                def _():
                    defect[...] = -coarse[:rows]

                @pl.when(band == 1)
                def _():
                    defect[...] = -coarse[margin:]
            else:
                defect[...] = -coarse[layers - first : layers - first + rows]

    for side in range(2):

        @pl.when(~has_band(side))
        def _():
            spots = pl.ds(side * (layers + rows), layers)
            cols[:, spots] = jnp.zeros((2, layers, width, 3 * channels), jnp.bfloat16)
            current[spots] = jnp.zeros((layers, width, channels), jnp.float32)

    state_load.wait()
    for side in range(2):

        @pl.when(has_band(side))
        def _():
            spots = pl.ds(layers + side * (rows - layers), layers)
            edge[side] = current[spots].astype(jnp.bfloat16)
            margin_copy(side).start()

    def load(row, carry):
        put(0, layers + row, current[layers + row])
        return carry

    lax.fori_loop(0, rows, load, 0)
    for side in range(2):

        @pl.when(has_band(side))
        def _():
            pltpu.make_async_remote_copy(
                src_ref=edge.at[1 - side],
                dst_ref=halo.at[0, side],
                send_sem=halo_send.at[0, 1 - side, 0],
                recv_sem=halo_recv.at[0, side, 0],
                device_id=(slab, band + 2 * side - 1),
                device_id_type=MESH,
            ).wait_recv()
            for at in range(layers):
                set_margin(0, side, at)

    for layer in range(layers):
        weight_load(layer).wait()
        layer_step(layer, True)
    defect[...] += current[own]

    near = 1 - lax.rem(band, 2)
    far = 1 - near

    def place(at):
        return near * (rows - 1) + (1 - 2 * near) * at

    def next_to(side):
        return (1 - side) * (layers - 1)

    @pl.when(slab == 0)
    def _():
        if slabs > 1:

            def hand_on(at, carry):
                row = place(at)
                send_row(row, current[layers + row])
                return carry

            lax.fori_loop(0, rows, hand_on, 0)
        first_load.wait()
        ends[...] = current[own]

    @pl.when(slab > 0)
    def _():
        def take_row(row):
            @pl.when(odd == 1)
            def _():
                wide_copy(row).wait_recv()

            @pl.when(odd == 0)
            def _():
                narrow_copy(row).wait_recv()
                inbox[row] = narrow_inbox[row].astype(jnp.float32)

            put(0, layers + row, inbox[row])

        take_row(place(0))
        take_cross(near, next_to(near))

        def chain(at, carry):
            row = place(at)

            @pl.when(at < rows - 1)
            def _():
                take_row(place(at + 1))

            @pl.when(at == rows - 1)
            def _():
                take_cross(far, next_to(far))

            slope_term = slope(0, layers + row - 1, 1, 0)
            value = inbox[row]

            @pl.when(slab < slabs - 1)
            def _():
                send_row(row, value + total_step * slope_term + defect[row])

            after = value + steps[0] * slope_term
            current[layers + row] = after
            put(1, layers + row, after)
            corrected[row] = value
            return carry

        lax.fori_loop(0, rows, chain, 0)
        if layers > 1:
            for side in range(2):
                for at in range(layers):
                    if at != next_to(side):
                        take_cross(side, at)

                @pl.when(has_band(side))
                def _():
                    first = 1 + side * (layers + rows - 1)
                    count = layers - 1
                    before = current[pl.ds(first, count)].reshape(count * width, channels)
                    after = before + steps[0] * slope(0, first - 1, count, 0)
                    current[pl.ds(first, count)] = after.reshape(count, width, channels)
                    put(1, first, after)

            for layer in range(1, layers):
                layer_step(layer, False)
        ends[...] = current[own]

    for side in range(2):

        @pl.when(has_band(side))
        def _():
            margin_copy(side).wait_send()

            @pl.when(slab < slabs - 1)
            def _():
                for at in range(layers):
                    cross_copy(side, at).wait_send()

    @pl.when((slab < slabs - 1) & (odd == 1))
    def _():
        for row in range(rows):
            narrow_copy(row).wait_send()

    @pl.when((slab < slabs - 1) & (odd == 0))
    def _():
        for row in range(rows):
            wide_copy(row).wait_send()


def local(start_states, weights, biases, step_sizes):
    rows, width, channels = start_states.shape[2:]
    layers = weights.shape[0]
    state = (rows, width, channels)
    anywhere = pl.BlockSpec(memory_space=pl.ANY)
    whole = pl.BlockSpec(memory_space=pltpu.VMEM)
    shape = jax.ShapeDtypeStruct(state, jnp.float32)
    corrected, ends = pl.pallas_call(
        functools.partial(kernel, lax.axis_size("fine"), lax.axis_size("coarse")),
        out_shape=(shape, shape),
        in_specs=[anywhere, anywhere, whole, pl.BlockSpec(memory_space=pltpu.SMEM)],
        out_specs=(whole, whole),
        scratch_shapes=[
            pltpu.VMEM((2, rows + 2 * layers, width, 3 * channels), jnp.bfloat16),
            pltpu.VMEM((rows + 2 * layers, width, channels), jnp.float32),
            pltpu.VMEM(state, jnp.float32),
            pltpu.VMEM(state, jnp.float32),
            pltpu.VMEM(state, jnp.float32),
            pltpu.VMEM(state, jnp.bfloat16),
            pltpu.VMEM(state, jnp.bfloat16),
            pltpu.VMEM((2, layers, width, channels), jnp.bfloat16),
            pltpu.VMEM((2, 2, layers, width, channels), jnp.bfloat16),
            pltpu.SemaphoreType.DMA((rows,)),
            pltpu.SemaphoreType.DMA((rows,)),
            pltpu.SemaphoreType.DMA((2, 2, layers)),
            pltpu.SemaphoreType.DMA((2, 2, layers)),
            pltpu.VMEM((layers, 9 * channels, channels), jnp.bfloat16),
            pltpu.SemaphoreType.DMA((layers + 2,)),
        ],
        compiler_params=pltpu.CompilerParams(
            collective_id=0, has_side_effects=True, vmem_limit_bytes=56 * 1024 * 1024
        ),
    )(
        start_states.reshape(state),
        weights.reshape(layers, 9 * channels, channels),
        biases,
        step_sizes,
    )
    return (corrected.reshape(start_states.shape), ends.reshape(start_states.shape))


def solution(mesh):
    in_specs = (
        P("fine", None, "coarse", None, None),
        P("fine", None, None, None),
        P("fine", None),
        P("fine"),
    )
    out_specs = (P("fine", None, "coarse", None, None), P("fine", None, "coarse", None, None))
    return jax.shard_map(local, mesh=mesh, in_specs=in_specs, out_specs=out_specs, check_vma=False)
```

time: 86.1 us -> 76.4 us (0.89)
  Pallas kernels: 81.5 us -> 71.8 us
    pallas_call x1, Pallas kernels: 81.5 us -> 71.8 us  [local(): pl.pallas_call(functools.partial(kernel, lax.axis_size('fine'), lax.axis_...]
where the time goes in v3:
time: 76.4 us; the launch traced here: 76.1 us
  Pallas kernels  71.8 us (94%)
  local copies, waits for them, and re-layouts  3.74 us (5%)
    pallas_call x1, Pallas kernels, local(): pl.pallas_call(functools.partial(kernel, lax.axis_size('fine'), lax.axis_...  71.8 us
    unnamed x2, local copies, waits for them, and re-layouts  3.74 us

profile of v3, /device:TPU:27, one launch (start us, length us, event | category | flops | bytes accessed | tf_op | source)
XLA Modules:
  0.0 76.1 jit_solution(15697014883468517573)
XLA Ops:
  0.6 71.8 %shard_map.59 = (f32[8,64,256]{2,1,0:T(8,128)}, f32[8,64,256]{2,1,0:T(8,128)}) custom-call(f32[8,64,256]{2,1,0:T(8,128)} %bitcast.5, bf16[4,2304,256]{2,1,0:T(8,128)(2,1)} %bitcast.4, f32[4,256]{1,0:T(4,128)} %biases.1, f32[4]{0:T(128)} %steps.1), custom_call_target="tpu_custom_call" | custom-call | tf_op jit(solution)/shard_map/pallas_call | solution.py:374
  72.4 1.9 %copy.8 = f32[1,1,8,64,256]{4,3,2,1,0:T(8,128)} copy(f32[1,1,8,64,256]{4,3,2,1,0:T(8,128)} %bitcast.7) | data formatting | bytes 1048576
  74.3 1.9 %copy.9 = f32[1,1,8,64,256]{4,3,2,1,0:T(8,128)} copy(f32[1,1,8,64,256]{4,3,2,1,0:T(8,128)} %bitcast.6) | data formatting | bytes 1048576

commit v4 on v3

--- a/solution.py
+++ b/solution.py
@@ -46,8 +46,7 @@
             stored_weights.at[layer], weights.at[layer], load_sem.at[layer]
         )
 
-    for layer in range(layers):
-        weight_load(layer).start()
+    weight_load(0).start()
 
     slab = lax.axis_index("fine")
     band = lax.axis_index("coarse")
@@ -256,6 +255,8 @@
 
     for layer in range(layers):
         weight_load(layer).wait()
+        if layer < layers - 1:
+            weight_load(layer + 1).start()
         layer_step(layer, True)
     defect[...] += current[own]
 
@@ -295,11 +296,21 @@
 
             put(0, layers + row, inbox[row])
 
+        def taps(row, first, count):
+            read = [cols[0, layers + row - 1 + first + a] for a in range(count)]
+            begin = pl.multiple_of(first * 3 * channels, 3 * channels)
+            return jnp.dot(
+                jnp.concatenate(read, axis=-1) if count > 1 else read[0],
+                weights[0, pl.ds(begin, count * 3 * channels)],
+                preferred_element_type=jnp.float32,
+            )
+
         take_row(place(0))
         take_cross(near, next_to(near))
 
         def chain(at, carry):
             row = place(at)
+            early = taps(row, near, 2)
 
             @pl.when(at < rows - 1)
             def _():
@@ -309,7 +320,7 @@
             def _():
                 take_cross(far, next_to(far))
 
-            slope_term = slope(0, layers + row - 1, 1, 0)
+            slope_term = jnp.tanh(early + taps(row, 2 * far, 1) + biases[0:1, :])
             value = inbox[row]
 
             @pl.when(slab < slabs - 1)
@@ -394,7 +405,7 @@
             pltpu.SemaphoreType.DMA((layers + 2,)),
         ],
         compiler_params=pltpu.CompilerParams(
-            collective_id=0, has_side_effects=True, vmem_limit_bytes=56 * 1024 * 1024
+            collective_id=0, has_side_effects=True, vmem_limit_bytes=52 * 1024 * 1024
         ),
     )(
         start_states.reshape(state),

time: 76.4 us -> 76.5 us (level)
    unnamed x2 -> x8, local copies, waits for them, and re-layouts: 3.74 us -> 3.96 us
where the time goes in v4:
time: 76.5 us; the launch traced here: 76.3 us
  Pallas kernels  71.6 us (94%)
  local copies, waits for them, and re-layouts  3.96 us (5%)
    pallas_call x1, Pallas kernels, local(): pl.pallas_call(functools.partial(kernel, lax.axis_size('fine'), lax.axis_...  71.6 us
    unnamed x8, local copies, waits for them, and re-layouts  3.96 us

profile of v4, /device:TPU:27, one launch (start us, length us, event | category | flops | bytes accessed | tf_op | source)
XLA Modules:
  0.0 76.3 jit_solution(6883608909325248195)
XLA Ops:
  0.6 0.0 copy-start
  0.6 1.0 %copy-done = f32[1,1,8,64,256]{4,3,2,1,0:T(8,128)S(1)} copy-done((f32[1,1,8,64,256]{4,3,2,1,0:T(8,128)S(1)}, f32[1,1,8,64,256]{4,3,2,1,0:T(8,128)}, u32[]{:S(2)}) %copy-start) | copy-done | bytes 524312
  1.7 0.0 copy-start.1
  1.7 0.7 copy-done.1
  2.4 0.0 copy-start.2
  2.4 0.7 copy-done.2
  3.0 71.6 %shard_map.59 = (f32[8,64,256]{2,1,0:T(8,128)S(1)}, f32[8,64,256]{2,1,0:T(8,128)S(1)}) custom-call(f32[8,64,256]{2,1,0:T(8,128)S(1)} %bitcast.4, bf16[4,2304,256]{2,1,0:T(8,128)(2,1)} %bitcast.7, f32[4,256]{1,0:T(4,128)S(1)} %copy-done.1, f32[4]{0:T(128)S(1)} %copy-done.2), custom_call_target="tpu_custom_call" | custom-call | tf_op jit(solution)/shard_map/pallas_call | solution.py:385
  74.7 0.8 %copy.8 = f32[1,1,8,64,256]{4,3,2,1,0:T(8,128)} copy(f32[1,1,8,64,256]{4,3,2,1,0:T(8,128)S(1)} %bitcast.6) | data formatting | bytes 1048576
  75.5 0.8 %copy.9 = f32[1,1,8,64,256]{4,3,2,1,0:T(8,128)} copy(f32[1,1,8,64,256]{4,3,2,1,0:T(8,128)S(1)} %bitcast.5) | data formatting | bytes 1048576
Async XLA Ops:
  0.6 1.0 %copy-start = (f32[1,1,8,64,256]{4,3,2,1,0:T(8,128)S(1)}, f32[1,1,8,64,256]{4,3,2,1,0:T(8,128)}, u32[]{:S(2)}) copy-start(f32[1,1,8,64,256]{4,3,2,1,0:T(8,128)} %param.4) | copy-start | bytes 1572868
  1.7 0.7 copy-start.1
  2.4 0.7 copy-start.2

commit v5 on v3

--- a/solution.py
+++ b/solution.py
@@ -38,6 +38,7 @@
     rows, width, channels = start.shape
     layers = weights.shape[0]
     own = pl.ds(layers, rows)
+    step = 2 if rows % 2 == 0 and layers % 2 == 0 else 1
     state_load = pltpu.make_async_copy(start, current.at[own], load_sem.at[layers])
     state_load.start()
 
@@ -46,8 +47,7 @@
             stored_weights.at[layer], weights.at[layer], load_sem.at[layer]
         )
 
-    for layer in range(layers):
-        weight_load(layer).start()
+    weight_load(0).start()
 
     slab = lax.axis_index("fine")
     band = lax.axis_index("coarse")
@@ -114,8 +114,8 @@
 
     def cross_copy(side, at):
         return pltpu.make_async_remote_copy(
-            src_ref=narrow.at[side * (rows - layers) + at],
-            dst_ref=halo.at[1, 1 - side, at],
+            src_ref=narrow.at[pl.ds(side * (rows - layers) + at, step)],
+            dst_ref=halo.at[1, 1 - side, pl.ds(at, step)],
             send_sem=halo_send.at[1, side, at],
             recv_sem=halo_recv.at[1, 1 - side, at],
             device_id=(slab + 1, band + 2 * side - 1),
@@ -124,8 +124,8 @@
 
     def wide_copy(row):
         return pltpu.make_async_remote_copy(
-            src_ref=advanced.at[row],
-            dst_ref=inbox.at[row],
+            src_ref=advanced.at[pl.ds(row, step)],
+            dst_ref=inbox.at[pl.ds(row, step)],
             send_sem=row_send.at[row],
             recv_sem=row_recv.at[row],
             device_id=(slab + 1, band),
@@ -134,8 +134,8 @@
 
     def narrow_copy(row):
         return pltpu.make_async_remote_copy(
-            src_ref=narrow.at[row],
-            dst_ref=narrow_inbox.at[row],
+            src_ref=narrow.at[pl.ds(row, step)],
+            dst_ref=narrow_inbox.at[pl.ds(row, step)],
             send_sem=row_send.at[row],
             recv_sem=row_recv.at[row],
             device_id=(slab + 1, band),
@@ -145,7 +145,7 @@
     odd = lax.rem(slab, 2)
 
     def send_row(row, value):
-        narrow[row] = value.astype(jnp.bfloat16)
+        narrow[pl.ds(row, step)] = value.astype(jnp.bfloat16)
 
         @pl.when(odd == 1)
         def _():
@@ -153,7 +153,7 @@
 
         @pl.when(odd == 0)
         def _():
-            advanced[row] = value
+            advanced[pl.ds(row, step)] = value
             wide_copy(row).start()
 
         for side in range(2):
@@ -173,14 +173,15 @@
         @pl.when(has_band(side))
         def _():
             pltpu.make_async_remote_copy(
-                src_ref=narrow.at[at],
-                dst_ref=halo.at[1, side, at],
+                src_ref=narrow.at[pl.ds(at, step)],
+                dst_ref=halo.at[1, side, pl.ds(at, step)],
                 send_sem=halo_send.at[1, 1 - side, at],
                 recv_sem=halo_recv.at[1, side, at],
                 device_id=(slab, band + 2 * side - 1),
                 device_id_type=MESH,
             ).wait_recv()
-            set_margin(1, side, at)
+            for more in range(step):
+                set_margin(1, side, at + more)
 
     def layer_step(layer, relaxing):
         margin = layers - 1 - layer
@@ -256,6 +257,8 @@
 
     for layer in range(layers):
         weight_load(layer).wait()
+        if layer < layers - 1:
+            weight_load(layer + 1).start()
         layer_step(layer, True)
     defect[...] += current[own]
 
@@ -263,10 +266,10 @@
     far = 1 - near
 
     def place(at):
-        return near * (rows - 1) + (1 - 2 * near) * at
+        return near * (rows - step) + (1 - 2 * near) * at * step
 
     def next_to(side):
-        return (1 - side) * (layers - 1)
+        return (1 - side) * (layers - step)
 
     @pl.when(slab == 0)
     def _():
@@ -274,10 +277,10 @@
 
             def hand_on(at, carry):
                 row = place(at)
-                send_row(row, current[layers + row])
+                send_row(row, current[pl.ds(layers + row, step)])
                 return carry
 
-            lax.fori_loop(0, rows, hand_on, 0)
+            lax.fori_loop(0, rows // step, hand_on, 0)
         first_load.wait()
         ends[...] = current[own]
 
@@ -291,41 +294,42 @@
             @pl.when(odd == 0)
             def _():
                 narrow_copy(row).wait_recv()
-                inbox[row] = narrow_inbox[row].astype(jnp.float32)
-
-            put(0, layers + row, inbox[row])
-
+                inbox[pl.ds(row, step)] = narrow_inbox[pl.ds(row, step)].astype(jnp.float32)
+
+            put(0, layers + row, inbox[pl.ds(row, step)].reshape(step * width, channels))
+
+        group = (step, width, channels)
         take_row(place(0))
         take_cross(near, next_to(near))
 
         def chain(at, carry):
             row = place(at)
 
-            @pl.when(at < rows - 1)
+            @pl.when(at < rows // step - 1)
             def _():
                 take_row(place(at + 1))
 
-            @pl.when(at == rows - 1)
+            @pl.when(at == rows // step - 1)
             def _():
                 take_cross(far, next_to(far))
 
-            slope_term = slope(0, layers + row - 1, 1, 0)
-            value = inbox[row]
+            slope_term = slope(0, layers + row - 1, step, 0).reshape(group)
+            value = inbox[pl.ds(row, step)]
 
             @pl.when(slab < slabs - 1)
             def _():
-                send_row(row, value + total_step * slope_term + defect[row])
+                send_row(row, value + total_step * slope_term + defect[pl.ds(row, step)])
 
             after = value + steps[0] * slope_term
-            current[layers + row] = after
-            put(1, layers + row, after)
-            corrected[row] = value
+            current[pl.ds(layers + row, step)] = after
+            put(1, layers + row, after.reshape(step * width, channels))
+            corrected[pl.ds(row, step)] = value
             return carry
 
-        lax.fori_loop(0, rows, chain, 0)
+        lax.fori_loop(0, rows // step, chain, 0)
         if layers > 1:
             for side in range(2):
-                for at in range(layers):
+                for at in range(0, layers, step):
                     if at != next_to(side):
                         take_cross(side, at)
 
@@ -350,17 +354,17 @@
 
             @pl.when(slab < slabs - 1)
             def _():
-                for at in range(layers):
+                for at in range(0, layers, step):
                     cross_copy(side, at).wait_send()
 
     @pl.when((slab < slabs - 1) & (odd == 1))
     def _():
-        for row in range(rows):
+        for row in range(0, rows, step):
             narrow_copy(row).wait_send()
 
     @pl.when((slab < slabs - 1) & (odd == 0))
     def _():
-        for row in range(rows):
+        for row in range(0, rows, step):
             wide_copy(row).wait_send()
 
 
@@ -394,7 +398,7 @@
             pltpu.SemaphoreType.DMA((layers + 2,)),
         ],
         compiler_params=pltpu.CompilerParams(
-            collective_id=0, has_side_effects=True, vmem_limit_bytes=56 * 1024 * 1024
+            collective_id=0, has_side_effects=True, vmem_limit_bytes=52 * 1024 * 1024
         ),
     )(
         start_states.reshape(state),

time: 76.4 us -> 83.1 us (1.088)
  Pallas kernels: 71.8 us -> 78.3 us
    pallas_call x1, Pallas kernels: 71.8 us -> 78.3 us  [local(): pl.pallas_call(functools.partial(kernel, lax.axis_size('fine'), lax.axis_...]
    unnamed x2 -> x8, local copies, waits for them, and re-layouts: 3.74 us -> 3.96 us
where the time goes in v5:
time: 83.1 us; the launch traced here: 82.9 us
  Pallas kernels  78.3 us (94%)
  local copies, waits for them, and re-layouts  3.96 us (5%)
    pallas_call x1, Pallas kernels, local(): pl.pallas_call(functools.partial(kernel, lax.axis_size('fine'), lax.axis_...  78.3 us
    unnamed x8, local copies, waits for them, and re-layouts  3.96 us

profile of v5, /device:TPU:27, one launch (start us, length us, event | category | flops | bytes accessed | tf_op | source)
XLA Modules:
  0.0 82.9 jit_solution(16126392802962026478)
XLA Ops:
  0.6 0.0 copy-start
  0.6 1.0 %copy-done = f32[1,1,8,64,256]{4,3,2,1,0:T(8,128)S(1)} copy-done((f32[1,1,8,64,256]{4,3,2,1,0:T(8,128)S(1)}, f32[1,1,8,64,256]{4,3,2,1,0:T(8,128)}, u32[]{:S(2)}) %copy-start) | copy-done | bytes 524312
  1.7 0.0 copy-start.1
  1.7 0.7 copy-done.1
  2.4 0.0 copy-start.2
  2.4 0.7 copy-done.2
  3.0 78.3 %shard_map.59 = (f32[8,64,256]{2,1,0:T(8,128)S(1)}, f32[8,64,256]{2,1,0:T(8,128)S(1)}) custom-call(f32[8,64,256]{2,1,0:T(8,128)S(1)} %bitcast.4, bf16[4,2304,256]{2,1,0:T(8,128)(2,1)} %bitcast.7, f32[4,256]{1,0:T(4,128)S(1)} %copy-done.1, f32[4]{0:T(128)S(1)} %copy-done.2), custom_call_target="tpu_custom_call" | custom-call | tf_op jit(solution)/shard_map/pallas_call | solution.py:378
  81.3 0.8 copy.8
  82.1 0.8 copy.9
Async XLA Ops:
  0.6 1.0 %copy-start = (f32[1,1,8,64,256]{4,3,2,1,0:T(8,128)S(1)}, f32[1,1,8,64,256]{4,3,2,1,0:T(8,128)}, u32[]{:S(2)}) copy-start(f32[1,1,8,64,256]{4,3,2,1,0:T(8,128)} %param.4) | copy-start | bytes 1572868
  1.7 0.7 copy-start.1
  2.4 0.7 copy-start.2
